TPU v7x, 32 devices: a whole 2x2x4 slice. The times are simulated.
32 devices in a mesh: dp: 8 (over z, y), tensor: 4 (over x, core).
Axes of the slice: x: 2, y: 2, z: 4, core: 2. Of those that a mesh axis runs over, the one named last changes fastest.
Arguments:
- tokens: bfloat16 [16384, 1024], P(('dp', 'tensor')), may hold values from -6 to 6
- cotangent: bfloat16 [16384, 1024], P(('dp', 'tensor')), may hold values from -6 to 6
- segments: int32 [16384], P('dp'), may hold values from 0 to 15, never falling along the last dimension, each value on 1 to 1920 neighbouring positions
- routes: int32 [16384, 8], P(('dp', 'tensor')), may hold values from 0 to 31, all different within a row; in each aligned block of 512 rows (0 to 511, 512 to 1023, ...) at most 144 rows name the same one
- gain_attn: bfloat16 [1024], P(('dp', 'tensor')), may hold values from 0.5 to 1.5
- w_query: bfloat16 [1024, 1024], P('dp', 'tensor'), may hold values from -0.1875 to 0.1875
- key_weight: bfloat16 [1024, 512], P('dp', 'tensor'), may hold values from -0.1875 to 0.1875
- value_weight: bfloat16 [1024, 512], P('dp', 'tensor'), may hold values from -0.1875 to 0.1875
- w_out: bfloat16 [1024, 1024], P('tensor', 'dp'), may hold values from -0.75 to 0.75
- gain_moe: bfloat16 [1024], P(('dp', 'tensor')), may hold values from 0.5 to 1.5
- w_router: bfloat16 [1024, 32], P(('dp', 'tensor')), may hold values from -0.09375 to 0.09375
- w_gate: bfloat16 [32, 1024, 512], P('tensor', 'dp'), may hold values from -0.1875 to 0.1875
- w_up: bfloat16 [32, 1024, 512], P('tensor', 'dp'), may hold values from -0.1875 to 0.1875
- w_down: bfloat16 [32, 512, 1024], P('tensor', None, 'dp'), may hold values from -0.75 to 0.75
Outputs:
- mixed_out: bfloat16 [16384, 1024], P(('dp', 'tensor'))
- grad_tokens: float32 [16384, 1024], P(('dp', 'tensor'))
- grad_gain_attn: float32 [1024], P(('dp', 'tensor'))
- grad_w_query: float32 [1024, 1024], P('dp', 'tensor')
- grad_w_key: float32 [1024, 512], P('dp', 'tensor')
- grad_w_value: float32 [1024, 512], P('dp', 'tensor')
- grad_w_out: float32 [1024, 1024], P('tensor', 'dp')
- grad_gain_moe: float32 [1024], P(('dp', 'tensor'))
- grad_w_router: float32 [1024, 32], P(('dp', 'tensor'))
- grad_w_gate: float32 [32, 1024, 512], P('tensor', 'dp')
- grad_w_up: float32 [32, 1024, 512], P('tensor', 'dp')
- grad_w_down: float32 [32, 512, 1024], P('tensor', None, 'dp')
Inputs may be any that keep to these rules, and one draw needn't show every extreme that they name: `segments`: segment numbers never fall along the tokens; a segment holds at most 1920 tokens, and one holds exactly that many. `routes`: each row names 8 different experts; in each aligned block of 512 rows (the rows of one device) no expert is named by more than 144 rows, a bound that some block reaches.
All inputs are finite; a program needn't handle non-finite values.
Results may differ from a plain program's by a relative error of at most 0.019.
Values may be sent and summed in bfloat16 or wider, within the bound.
A program may use at most 256 MiB of HBM per device.

v0:
```python
import math

import jax
import jax.numpy as jnp
from jax import lax
from jax.sharding import PartitionSpec as P

HEAD_DIM = 64
E = 32
TOPK = 8
SEQUENCE_LENGTH = 2048


HIGHEST = lax.Precision.HIGHEST
EPSILON = 1e-06
ROTARY_BASE = 10000.0
MASKED_SCORE = -1e30


def rms_forward(values, gain):
    factor = lax.rsqrt(jnp.mean(values * values, axis=-1, keepdims=True) + EPSILON)
    return (values * factor * gain, factor)


def rms_backward(values, factor, gain, grad):
    normal = values * factor
    gain_grad = jnp.sum(grad * normal, axis=0)
    inner = grad * gain
    back = factor * (inner - normal * jnp.mean(inner * normal, axis=-1, keepdims=True))
    return (back, gain_grad)


def positions_of(segment_rows):
    length = segment_rows.shape[1]
    place = jnp.arange(length, dtype=jnp.int32)
    shifted = jnp.concatenate([segment_rows[:, :1], segment_rows[:, :-1]], axis=1)
    opening = (place[None, :] == 0) | (segment_rows != shifted)
    begin = lax.cummax(jnp.where(opening, place[None, :], 0), axis=1)
    return place[None, :] - begin


def rotary_tables(position, head_size):
    half_size = head_size // 2
    frequency = jnp.exp(
        jnp.arange(half_size, dtype=jnp.float32) * (-2.0 * math.log(ROTARY_BASE) / head_size)
    )
    angle = position.astype(jnp.float32)[:, None] * frequency[None, :]
    return (jnp.cos(angle), jnp.sin(angle))


def apply_rotary(values, cosine_table, sine_values):
    half_size = values.shape[-1] // 2
    front_half = values[..., :half_size]
    back_half = values[..., half_size:]
    cos_b = cosine_table[:, None, :]
    sin_b = sine_values[:, None, :]
    return jnp.concatenate(
        [front_half * cos_b - back_half * sin_b, back_half * cos_b + front_half * sin_b], axis=-1
    )


def unrotate(grad, cosine_table, sine_values):
    half_size = grad.shape[-1] // 2
    front_half = grad[..., :half_size]
    back_half = grad[..., half_size:]
    cos_b = cosine_table[:, None, :]
    sin_b = sine_values[:, None, :]
    return jnp.concatenate(
        [front_half * cos_b + back_half * sin_b, back_half * cos_b - front_half * sin_b], axis=-1
    )


def masked_scores(query_block, key_matrix, query_segments, key_segments, offset, score_scale):
    raw_scores = (
        jnp.einsum("qcgd,kcd->cgqk", query_block, key_matrix, preferred_element_type=jnp.float32)
        * score_scale
    )
    query_place = offset + jnp.arange(query_block.shape[0])
    key_place = jnp.arange(key_matrix.shape[0])
    allowed = (query_segments[:, None] == key_segments[None, :]) & (
        key_place[None, :] <= query_place[:, None]
    )
    return jnp.where(allowed, raw_scores, MASKED_SCORE)


def attend_forward(queries, key_matrix, value_matrix, segment_ids, block_rows, score_scale):
    length = queries.shape[0]

    def one_block(block_index):
        offset = block_index * block_rows
        query_block = lax.dynamic_slice_in_dim(queries, offset, block_rows, 0)
        query_segments = lax.dynamic_slice_in_dim(segment_ids, offset, block_rows, 0)
        scores = masked_scores(
            query_block, key_matrix, query_segments, segment_ids, offset, score_scale
        )
        row_max = jnp.max(scores, axis=-1, keepdims=True)
        log_total = jnp.log(jnp.sum(jnp.exp(scores - row_max), axis=-1, keepdims=True)) + row_max
        rounded = jnp.exp(scores - log_total).astype(jnp.bfloat16)
        result = jnp.einsum(
            "cgqk,kcd->qcgd", rounded, value_matrix, preferred_element_type=jnp.float32
        )
        return (result.astype(jnp.bfloat16), log_total[..., 0])

    outputs, log_totals = lax.map(one_block, jnp.arange(length // block_rows))
    return (outputs.reshape((length,) + queries.shape[1:]), log_totals)


def attend_backward(
    queries, key_matrix, value_matrix, segment_ids, log_totals, mix_grad, block_rows, score_scale
):
    length = queries.shape[0]

    def one_block(running, block_index):
        key_grad, value_grad = running
        offset = block_index * block_rows
        query_block = lax.dynamic_slice_in_dim(queries, offset, block_rows, 0)
        query_segments = lax.dynamic_slice_in_dim(segment_ids, offset, block_rows, 0)
        grad_block = lax.dynamic_slice_in_dim(mix_grad, offset, block_rows, 0)
        scores = masked_scores(
            query_block, key_matrix, query_segments, segment_ids, offset, score_scale
        )
        softmaxed = jnp.exp(scores - log_totals[block_index][..., None])
        rounded = softmaxed.astype(jnp.bfloat16)
        prob_grad = jnp.einsum(
            "qcgd,kcd->cgqk", grad_block, value_matrix, preferred_element_type=jnp.float32
        )
        score_grad = (
            softmaxed * (prob_grad - jnp.sum(softmaxed * prob_grad, axis=-1, keepdims=True))
        ).astype(jnp.bfloat16)
        query_grad = (
            jnp.einsum("cgqk,kcd->qcgd", score_grad, key_matrix, preferred_element_type=jnp.float32)
            * score_scale
        )
        key_grad = (
            key_grad
            + jnp.einsum(
                "cgqk,qcgd->kcd", score_grad, query_block, preferred_element_type=jnp.float32
            )
            * score_scale
        )
        value_grad = value_grad + jnp.einsum(
            "cgqk,qcgd->kcd", rounded, grad_block, preferred_element_type=jnp.float32
        )
        return ((key_grad, value_grad), query_grad)

    empty = jnp.zeros(key_matrix.shape, jnp.float32)
    (key_grad, value_grad), query_grad = lax.scan(
        one_block, (empty, empty), jnp.arange(length // block_rows)
    )
    return (query_grad.reshape(queries.shape), key_grad, value_grad)


def expert_forward(batch_rows, gate_w, up_w, down_w):
    pre_gate = jnp.dot(batch_rows, gate_w, preferred_element_type=jnp.float32)
    pre_up = jnp.dot(batch_rows, up_w, preferred_element_type=jnp.float32)
    activation = (jax.nn.silu(pre_gate) * pre_up).astype(jnp.bfloat16)
    return jnp.dot(activation, down_w, preferred_element_type=jnp.float32).astype(jnp.bfloat16)


def expert_backward(batch_rows, out_grad, gate_w, up_w, down_w):
    pre_gate = jnp.dot(batch_rows, gate_w, preferred_element_type=jnp.float32)
    pre_up = jnp.dot(batch_rows, up_w, preferred_element_type=jnp.float32)
    sigmoid_gate = jax.nn.sigmoid(pre_gate)
    silu_gate = pre_gate * sigmoid_gate
    activation = (silu_gate * pre_up).astype(jnp.bfloat16)
    down_grad = jnp.einsum("rf,rd->fd", activation, out_grad, preferred_element_type=jnp.float32)
    act_grad = jnp.einsum("rd,fd->rf", out_grad, down_w, preferred_element_type=jnp.float32)
    gate_grad = (act_grad * pre_up * sigmoid_gate * (1.0 + pre_gate * (1.0 - sigmoid_gate))).astype(
        jnp.bfloat16
    )
    up_grad = (act_grad * silu_gate).astype(jnp.bfloat16)
    gate_w_grad = jnp.einsum("rd,rf->df", batch_rows, gate_grad, preferred_element_type=jnp.float32)
    up_w_grad = jnp.einsum("rd,rf->df", batch_rows, up_grad, preferred_element_type=jnp.float32)
    row_grad = jnp.einsum("rf,df->rd", gate_grad, gate_w, preferred_element_type=jnp.float32)
    row_grad = row_grad + jnp.einsum("rf,df->rd", up_grad, up_w, preferred_element_type=jnp.float32)
    return (row_grad.astype(jnp.bfloat16), gate_w_grad, up_w_grad, down_grad)


def to_owner(outgoing):
    return lax.all_to_all(outgoing, "tensor", split_axis=0, concat_axis=2, tiled=True)[0]


def to_source(stacked):
    return lax.all_to_all(stacked[None], "tensor", split_axis=2, concat_axis=0, tiled=True)


def fetch_expert(gate_part, up_part, down_part):
    return (
        lax.all_gather(gate_part, "dp", axis=0, tiled=True),
        lax.all_gather(up_part, "dp", axis=0, tiled=True),
        lax.all_gather(down_part, "dp", axis=1, tiled=True),
    )


def fetch_again(gate_part, up_part, down_part):
    return (
        lax.all_gather(gate_part, "dp", axis=0, tiled=True),
        lax.all_gather(up_part, "dp", axis=0, tiled=True),
        lax.all_gather(down_part, "dp", axis=1, tiled=True),
    )


def per_device(
    tokens,
    cotangent,
    segments,
    routes,
    gain_attn,
    w_query,
    key_weight,
    value_weight,
    w_out,
    gain_moe,
    w_router,
    w_gate,
    w_up,
    w_down,
):
    groups = lax.axis_size("tensor")
    row_total, model_width = tokens.shape
    token_total = segments.shape[0]
    seq_count = token_total // SEQUENCE_LENGTH
    block_rows = min(512, SEQUENCE_LENGTH)
    score_scale = HEAD_DIM ** (-0.5)
    local_experts = w_gate.shape[0]
    capacity = max(2, row_total * TOPK * 9 // (8 * E))
    slot_total = row_total * TOPK
    gain_a, gain_m, router = (
        lax.all_gather(gain_attn, ("dp", "tensor"), axis=0, tiled=True),
        lax.all_gather(gain_moe, ("dp", "tensor"), axis=0, tiled=True),
        lax.all_gather(w_router, ("dp", "tensor"), axis=0, tiled=True),
    )
    query_w, key_w, value_w, out_w = (
        lax.all_gather(w_query, "dp", axis=0, tiled=True),
        lax.all_gather(key_weight, "dp", axis=0, tiled=True),
        lax.all_gather(value_weight, "dp", axis=0, tiled=True),
        lax.all_gather(w_out, "dp", axis=1, tiled=True),
    )
    gain_a32 = gain_a.astype(jnp.float32)
    gain_m32 = gain_m.astype(jnp.float32)
    kv_heads = key_w.shape[1] // HEAD_DIM
    q_heads = query_w.shape[1] // HEAD_DIM
    head_share = q_heads // kv_heads
    inputs = tokens.astype(jnp.float32)
    normed_rows, factor_a = rms_forward(inputs, gain_a32)
    gathered = lax.all_gather(normed_rows.astype(jnp.bfloat16), "tensor", axis=0, tiled=True)
    segment_rows = segments.reshape(seq_count, SEQUENCE_LENGTH)
    cosine_table, sine_values = rotary_tables(
        positions_of(segment_rows).reshape(token_total), HEAD_DIM
    )
    query_lin = jnp.dot(gathered, query_w, preferred_element_type=jnp.float32).reshape(
        token_total, q_heads, HEAD_DIM
    )
    key_linear = jnp.dot(gathered, key_w, preferred_element_type=jnp.float32).reshape(
        token_total, kv_heads, HEAD_DIM
    )
    value_matrix = (
        jnp.dot(gathered, value_w, preferred_element_type=jnp.float32)
        .astype(jnp.bfloat16)
        .reshape(seq_count, SEQUENCE_LENGTH, kv_heads, HEAD_DIM)
    )
    queries = (
        apply_rotary(query_lin, cosine_table, sine_values)
        .astype(jnp.bfloat16)
        .reshape(seq_count, SEQUENCE_LENGTH, kv_heads, head_share, HEAD_DIM)
    )
    key_matrix = (
        apply_rotary(key_linear, cosine_table, sine_values)
        .astype(jnp.bfloat16)
        .reshape(seq_count, SEQUENCE_LENGTH, kv_heads, HEAD_DIM)
    )

    def forward_sequence(inputs_seq):
        return attend_forward(
            inputs_seq[0], inputs_seq[1], inputs_seq[2], inputs_seq[3], block_rows, score_scale
        )

    mixed, log_totals = lax.map(forward_sequence, (queries, key_matrix, value_matrix, segment_rows))
    mixed = mixed.reshape(token_total, q_heads * HEAD_DIM)
    hidden = inputs + lax.psum_scatter(
        jnp.dot(mixed, out_w, preferred_element_type=jnp.float32),
        "tensor",
        scatter_dimension=0,
        tiled=True,
    )
    normed_moe, factor_m = rms_forward(hidden, gain_m32)
    low_moe = normed_moe.astype(jnp.bfloat16)
    logits = jnp.dot(low_moe, router, preferred_element_type=jnp.float32)
    expert_ids = jnp.arange(E, dtype=jnp.int32)
    picker = (routes[:, :, None] == expert_ids[None, None, :]).astype(jnp.float32)
    gates = jax.nn.softmax(jnp.sum(picker * logits[:, None, :], axis=2), axis=-1)
    flat_routes = routes.reshape(slot_total)
    matches = (flat_routes[:, None] == expert_ids[None, :]).astype(jnp.int32)
    slot_rank = jnp.sum(
        matches * (jnp.cumsum(matches, axis=0, dtype=jnp.int32) - 1), axis=1, dtype=jnp.int32
    )
    slot_of = flat_routes * capacity + slot_rank
    source = (
        jnp.full((E * capacity,), slot_total, jnp.int32)
        .at[slot_of]
        .set(jnp.arange(slot_total, dtype=jnp.int32))
    )
    padded = jnp.concatenate([low_moe, jnp.zeros((1, model_width), jnp.bfloat16)], axis=0)
    received = to_owner(
        padded[source // TOPK].reshape(groups, local_experts, capacity, model_width)
    )
    fetched = []
    outputs = []
    for expert_index in range(local_experts):
        weights = fetch_expert(w_gate[expert_index], w_up[expert_index], w_down[expert_index])
        fetched.append(weights)
        outputs.append(expert_forward(received[expert_index], weights[0], weights[1], weights[2]))
    returned = to_source(jnp.stack(outputs)).reshape(E * capacity, model_width)
    assigned = returned[slot_of].reshape(row_total, TOPK, model_width)
    moe_sum = hidden
    for choice_index in range(TOPK):
        moe_sum = moe_sum + gates[:, choice_index : choice_index + 1] * assigned[
            :, choice_index
        ].astype(jnp.float32)
    mixed_out = moe_sum.astype(jnp.bfloat16)
    grad_out = cotangent.astype(jnp.float32)
    gate_grad = jnp.stack(
        [
            jnp.sum(grad_out * assigned[:, choice_index].astype(jnp.float32), axis=-1)
            for choice_index in range(TOPK)
        ],
        axis=1,
    )
    pick_grad = gates * (gate_grad - jnp.sum(gates * gate_grad, axis=-1, keepdims=True))
    logit_grad = jnp.sum(picker * pick_grad[:, :, None], axis=1)
    copy_out_grad = (
        (gates[:, :, None] * grad_out[:, None, :])
        .astype(jnp.bfloat16)
        .reshape(slot_total, model_width)
    )
    padded_grad = jnp.concatenate(
        [copy_out_grad, jnp.zeros((1, model_width), jnp.bfloat16)], axis=0
    )
    grad_received = to_owner(
        padded_grad[source].reshape(groups, local_experts, capacity, model_width)
    )
    back_rows = []
    gate_shares = []
    up_shares = []
    down_shares = []
    for expert_index in range(local_experts):
        weights = fetch_again(w_gate[expert_index], w_up[expert_index], w_down[expert_index])
        row_grad, gate_w_grad, up_w_grad, down_w_grad = expert_backward(
            received[expert_index], grad_received[expert_index], weights[0], weights[1], weights[2]
        )
        back_rows.append(row_grad)
        gate_share, up_share, down_share = (
            lax.psum_scatter(
                gate_w_grad.astype(jnp.bfloat16), "dp", scatter_dimension=0, tiled=True
            ).astype(jnp.float32),
            lax.psum_scatter(
                up_w_grad.astype(jnp.bfloat16), "dp", scatter_dimension=0, tiled=True
            ).astype(jnp.float32),
            lax.psum_scatter(
                down_w_grad.astype(jnp.bfloat16), "dp", scatter_dimension=1, tiled=True
            ).astype(jnp.float32),
        )
        gate_shares.append(gate_share)
        up_shares.append(up_share)
        down_shares.append(down_share)
    row_back = to_source(jnp.stack(back_rows)).reshape(E * capacity, model_width)
    copy_grad = row_back[slot_of].reshape(row_total, TOPK, model_width)
    norm_moe_grad = jnp.dot(logit_grad, router.astype(jnp.float32).T, precision=HIGHEST)
    for choice_index in range(TOPK):
        norm_moe_grad = norm_moe_grad + copy_grad[:, choice_index].astype(jnp.float32)
    router_grad = jnp.dot(low_moe.astype(jnp.float32).T, logit_grad, precision=HIGHEST)
    hidden_back, gain_m_grad = rms_backward(hidden, factor_m, gain_m32, norm_moe_grad)
    hidden_grad = grad_out + hidden_back
    branch_grad = lax.all_gather(hidden_grad.astype(jnp.bfloat16), "tensor", axis=0, tiled=True)
    out_w_grad = jnp.einsum("ti,td->id", mixed, branch_grad, preferred_element_type=jnp.float32)
    mix_grad = jnp.einsum(
        "td,id->ti", branch_grad, out_w, preferred_element_type=jnp.float32
    ).astype(jnp.bfloat16)
    mix_grad = mix_grad.reshape(seq_count, SEQUENCE_LENGTH, kv_heads, head_share, HEAD_DIM)

    def backward_sequence(inputs_seq):
        return attend_backward(
            inputs_seq[0],
            inputs_seq[1],
            inputs_seq[2],
            inputs_seq[3],
            inputs_seq[4],
            inputs_seq[5],
            block_rows,
            score_scale,
        )

    query_grad, key_grad, value_grad = lax.map(
        backward_sequence, (queries, key_matrix, value_matrix, segment_rows, log_totals, mix_grad)
    )
    query_lin_grad = (
        unrotate(query_grad.reshape(token_total, q_heads, HEAD_DIM), cosine_table, sine_values)
        .astype(jnp.bfloat16)
        .reshape(token_total, q_heads * HEAD_DIM)
    )
    key_lin_grad = (
        unrotate(key_grad.reshape(token_total, kv_heads, HEAD_DIM), cosine_table, sine_values)
        .astype(jnp.bfloat16)
        .reshape(token_total, kv_heads * HEAD_DIM)
    )
    value_low_grad = value_grad.astype(jnp.bfloat16).reshape(token_total, kv_heads * HEAD_DIM)
    query_w_grad = jnp.einsum(
        "td,th->dh", gathered, query_lin_grad, preferred_element_type=jnp.float32
    )
    key_w_grad = jnp.einsum("td,th->dh", gathered, key_lin_grad, preferred_element_type=jnp.float32)
    value_w_grad = jnp.einsum(
        "td,th->dh", gathered, value_low_grad, preferred_element_type=jnp.float32
    )
    summed = jnp.einsum("th,dh->td", query_lin_grad, query_w, preferred_element_type=jnp.float32)
    summed = summed + jnp.einsum(
        "th,dh->td", key_lin_grad, key_w, preferred_element_type=jnp.float32
    )
    norm_attn_grad = lax.psum_scatter(
        (
            summed
            + jnp.einsum("th,dh->td", value_low_grad, value_w, preferred_element_type=jnp.float32)
        ).astype(jnp.bfloat16),
        "tensor",
        scatter_dimension=0,
        tiled=True,
    ).astype(jnp.float32)
    input_back, gain_a_grad = rms_backward(inputs, factor_a, gain_a32, norm_attn_grad)
    input_grad = hidden_grad + input_back
    query_share, key_share, value_share, out_share = (
        lax.psum_scatter(
            query_w_grad.astype(jnp.bfloat16), "dp", scatter_dimension=0, tiled=True
        ).astype(jnp.float32),
        lax.psum_scatter(
            key_w_grad.astype(jnp.bfloat16), "dp", scatter_dimension=0, tiled=True
        ).astype(jnp.float32),
        lax.psum_scatter(
            value_w_grad.astype(jnp.bfloat16), "dp", scatter_dimension=0, tiled=True
        ).astype(jnp.float32),
        lax.psum_scatter(
            out_w_grad.astype(jnp.bfloat16), "dp", scatter_dimension=1, tiled=True
        ).astype(jnp.float32),
    )
    gain_a_share, gain_m_share, router_share = (
        lax.psum_scatter(gain_a_grad, ("dp", "tensor"), scatter_dimension=0, tiled=True),
        lax.psum_scatter(gain_m_grad, ("dp", "tensor"), scatter_dimension=0, tiled=True),
        lax.psum_scatter(router_grad, ("dp", "tensor"), scatter_dimension=0, tiled=True),
    )
    return (
        mixed_out,
        input_grad,
        gain_a_share,
        query_share,
        key_share,
        value_share,
        out_share,
        gain_m_share,
        router_share,
        jnp.stack(gate_shares),
        jnp.stack(up_shares),
        jnp.stack(down_shares),
    )


def solution(mesh):
    placed = (
        P(("dp", "tensor"), None),
        P(("dp", "tensor"), None),
        P("dp"),
        P(("dp", "tensor"), None),
        P(("dp", "tensor")),
        P("dp", "tensor"),
        P("dp", "tensor"),
        P("dp", "tensor"),
        P("tensor", "dp"),
        P(("dp", "tensor")),
        P(("dp", "tensor"), None),
        P("tensor", "dp", None),
        P("tensor", "dp", None),
        P("tensor", None, "dp"),
    )
    return jax.shard_map(
        per_device,
        mesh=mesh,
        in_specs=placed,
        out_specs=(
            P(("dp", "tensor"), None),
            P(("dp", "tensor"), None),
            P(("dp", "tensor")),
            P("dp", "tensor"),
            P("dp", "tensor"),
            P("dp", "tensor"),
            P("tensor", "dp"),
            P(("dp", "tensor")),
            P(("dp", "tensor"), None),
            P("tensor", "dp", None),
            P("tensor", "dp", None),
            P("tensor", None, "dp"),
        ),
        check_vma=False,
    )
```

profile of v0, /device:TPU:0, one launch (start us, length us, event | category | flops | bytes accessed | tf_op | source)
XLA Modules:
  0.0 3934.1 jit_solution(4978885310274865452)
XLA Ops:
  9.8 42.0 %all-reduce.7 = (bf16[1024]{0:T(1024)(128)(2,1)S(1)}, bf16[1024]{0:T(1024)(128)(2,1)S(1)}) all-reduce(bf16[1024]{0:T(1024)(128)(2,1)S(1)} %dynamic-update-slice, bf16[1024]{0:T(1024)(128)(2,1)S(1)} %dynamic-update-slice.1), channel_id=1, replica_groups=mesh['dp'=8,'tensor'=4] {'dp','tensor'}, use_global_device_ids=true, to_apply=%add.2 | all-reduce | flops 2048 | bytes 8192
  187.5 64.5 %while.47 = (s32[]{:T(128)}, bf16[4,512,2,2,64]{1,4,3,2,0:T(8,128)(2,1)S(1)}, f32[4,2,2,512]{3,2,1,0:T(2,128)}, s32[4]{0:T(128)S(1)}, s32[2048]{0:T(1024)S(1)}, ...) while((s32[]{:T(128)}, ...), condition=%wide.region_6.7_spmd, body=%wide.region_3.6_spmd.sunk | while | flops 1123154432 | bytes 56182984 | solution.py:104
  356.2 101.9 %all-to-all-done = bf16[4,8,144,1024]{3,2,1,0:T(8,128)(2,1)} async-done(((bf16[4,8,144,1024]{3,2,1,0:T(8,128)(2,1)}), bf16[4,8,144,1024]{3,2,1,0:T(8,128)(2,1)}, u32[]{:S(2)}, u32[]{:S(2)}) %all-to-all-start) | async-done | bytes 9437216 | tf_op jit(solution)/shard_map/all_to_all | solution.py:180
  510.5 37.7 all-gather.69.cloned.1.call-done
  552.2 37.8 all-gather.73.cloned.1.call-done
  593.4 37.8 all-gather.75.cloned.1.call-done
  635.2 37.8 all-gather.79.cloned.1.call-done
  676.5 37.7 all-gather.81.cloned.1.call-done
  718.2 37.9 all-gather.85.cloned.1.call-done
  759.1 38.1 all-gather.87.cloned.1.call-done
  840.8 37.6 all-gather.71.cloned.1.call-done
  881.5 37.8 all-gather.77.cloned.1.call-done
  922.2 37.8 all-gather.83.cloned.1.call-done
  963.1 37.7 all-gather.89.cloned.1.call-done
  1003.9 38.6 all-gather.91.cloned.1.call-done
  1045.5 38.3 all-gather.93.cloned.1.call-done
  1127.2 39.0 all-gather.97.cloned.1.call-done
  1169.2 38.2 all-gather.99.cloned.1.call-done
  1270.9 134.1 %all_gather.130 = bf16[1024,32]{1,0:T(8,128)(2,1)S(1)} all-gather(bf16[32,32]{1,0:T(8,128)(2,1)S(1)} %copy-done.132), channel_id=1, replica_groups=mesh['dp'=8,'tensor'=4] {'dp','tensor'}, dimensions={0}, use_global_device_ids=true | all-gather | bytes 67584 | tf_op jit(solution)/shard_map/all_gather | solution.py:231
  1444.7 39.1 fusion.224
  1533.4 108.5 %all_to_all.60 = bf16[4,8,144,1024]{3,2,1,0:T(8,128)(2,1)S(1)} all-to-all(bf16[4,8,144,1024]{3,2,1,0:T(8,128)(2,1)} %bitcast.772), channel_id=1, replica_groups=mesh['dp'=8,'tensor'=4] {'tensor'}, dimensions={0} | all-to-all | bytes 18874368 | tf_op jit(solution)/shard_map/all_to_all | solution.py:180
  1707.9 103.9 %all-to-all-done.3 = bf16[1,8,576,1024]{3,1,0,2:T(8,128)(2,1)} async-done(((bf16[1,8,576,1024]{3,1,0,2:T(8,128)(2,1)}), bf16[1,8,576,1024]{3,1,0,2:T(8,128)(2,1)}, u32[]{:S(2)}, u32[]{:S(2)}) %all-to-all-start.3) | async-done | bytes 9437216 | tf_op jit(solution)/shard_map/all_to_all | solution.py:184
  1850.4 38.6 fusion.223
  1979.3 290.9 %while.48 = (s32[]{:T(128)}, f32[2048,2,64]{0,2,1:T(8,128)}, f32[2048,2,64]{0,2,1:T(8,128)}, f32[4,512,2,2,64]{1,0,4,3,2:T(4,128)}, s32[4]{0:T(128)S(1)}, /*inde...) while((s32[]{:T(128)}, f32[2048,2,64]{0,2,1:T(8,128)}, ...), condition=%wide.region_29.30_spmd.clone, body=%wide.region_27.29_spmd.clone.sunk | while | flops 2751855104 | bytes 225520144 | solution.py:147
  2363.7 64.9 %reduce-scatter.76.cloned.1.call-done = bf16[128,512]{1,0:T(8,128)(2,1)} async-done(((bf16[1024,512]{1,0:T(8,128)(2,1)}), bf16[128,512]{1,0:T(8,128)(2,1)}) %reduce-scatter.76.cloned.1.call-update) | async-done | bytes 131088 | tf_op jit(solution)/shard_map/reduce_scatter | solution.py:353
  2431.2 63.9 %reduce-scatter.78.cloned.1.call-done = bf16[128,512]{1,0:T(8,128)(2,1)} async-done(((bf16[1024,512]{1,0:T(8,128)(2,1)}), bf16[128,512]{1,0:T(8,128)(2,1)}) %reduce-scatter.78.cloned.1.call-update) | async-done | bytes 131088 | tf_op jit(solution)/shard_map/reduce_scatter | solution.py:356
  2495.9 64.9 %reduce-scatter.80.cloned.1.call-done = bf16[128,512]{1,0:T(8,128)(2,1)} async-done(((bf16[1024,512]{1,0:T(8,128)(2,1)}), bf16[128,512]{1,0:T(8,128)(2,1)}) %reduce-scatter.80.cloned.1.call-update) | async-done | bytes 131088 | tf_op jit(solution)/shard_map/reduce_scatter | solution.py:356
  2561.8 65.3 %reduce-scatter.82.cloned.1.call-done = bf16[128,512]{1,0:T(8,128)(2,1)} async-done(((bf16[1024,512]{1,0:T(8,128)(2,1)}), bf16[128,512]{1,0:T(8,128)(2,1)}) %reduce-scatter.82.cloned.1.call-update) | async-done | bytes 131088 | tf_op jit(solution)/shard_map/reduce_scatter | solution.py:356
  2628.0 65.1 %reduce-scatter.84.cloned.1.call-done = bf16[128,512]{1,0:T(8,128)(2,1)} async-done(((bf16[1024,512]{1,0:T(8,128)(2,1)}), bf16[128,512]{1,0:T(8,128)(2,1)}) %reduce-scatter.84.cloned.1.call-update) | async-done | bytes 131088 | tf_op jit(solution)/shard_map/reduce_scatter | solution.py:356
  2694.0 65.5 %reduce-scatter.86.cloned.1.call-done = bf16[128,512]{1,0:T(8,128)(2,1)} async-done(((bf16[1024,512]{1,0:T(8,128)(2,1)}), bf16[128,512]{1,0:T(8,128)(2,1)}) %reduce-scatter.86.cloned.1.call-update) | async-done | bytes 131088 | tf_op jit(solution)/shard_map/reduce_scatter | solution.py:356
  2760.4 64.9 %reduce-scatter.88.cloned.1.call-done = bf16[128,512]{1,0:T(8,128)(2,1)} async-done(((bf16[1024,512]{1,0:T(8,128)(2,1)}), bf16[128,512]{1,0:T(8,128)(2,1)}) %reduce-scatter.88.cloned.1.call-update) | async-done | bytes 131088 | tf_op jit(solution)/shard_map/reduce_scatter | solution.py:356
  2826.3 65.5 %reduce-scatter.90.cloned.1.call-done = bf16[128,512]{1,0:T(8,128)(2,1)} async-done(((bf16[1024,512]{1,0:T(8,128)(2,1)}), bf16[128,512]{1,0:T(8,128)(2,1)}) %reduce-scatter.90.cloned.1.call-update) | async-done | bytes 131088 | tf_op jit(solution)/shard_map/reduce_scatter | solution.py:356
  2892.7 64.9 %reduce-scatter.92.cloned.1.call-done = bf16[128,512]{1,0:T(8,128)(2,1)} async-done(((bf16[1024,512]{1,0:T(8,128)(2,1)}), bf16[128,512]{1,0:T(8,128)(2,1)}) %reduce-scatter.92.cloned.1.call-update) | async-done | bytes 131088 | tf_op jit(solution)/shard_map/reduce_scatter | solution.py:356
  2960.1 63.7 %reduce-scatter.96.cloned.1.call-done = bf16[128,512]{1,0:T(8,128)(2,1)} async-done(((bf16[1024,512]{1,0:T(8,128)(2,1)}), bf16[128,512]{1,0:T(8,128)(2,1)}) %reduce-scatter.96.cloned.1.call-update) | async-done | bytes 131088
  3025.5 64.2 %reduce-scatter.98.cloned.1.call-done = bf16[128,512]{1,0:T(8,128)(2,1)} async-done(((bf16[1024,512]{1,0:T(8,128)(2,1)}), bf16[128,512]{1,0:T(8,128)(2,1)}) %reduce-scatter.98.cloned.1.call-update) | async-done | bytes 131088
  3090.8 65.3 %reduce-scatter.100.cloned.1.call-done = bf16[128,512]{1,0:T(8,128)(2,1)} async-done(((bf16[1024,512]{1,0:T(8,128)(2,1)}), bf16[128,512]{1,0:T(8,128)(2,1)}) %reduce-scatter.100.cloned.1.call-update) | async-done | bytes 131088
  3157.1 64.8 %reduce-scatter.102.cloned.1.call-done = bf16[128,512]{1,0:T(8,128)(2,1)} async-done(((bf16[1024,512]{1,0:T(8,128)(2,1)}), bf16[128,512]{1,0:T(8,128)(2,1)}) %reduce-scatter.102.cloned.1.call-update) | async-done | bytes 131088
  3223.0 65.3 %reduce-scatter.104.cloned.1.call-done = bf16[128,512]{1,0:T(8,128)(2,1)} async-done(((bf16[1024,512]{1,0:T(8,128)(2,1)}), bf16[128,512]{1,0:T(8,128)(2,1)}) %reduce-scatter.104.cloned.1.call-update) | async-done | bytes 131088
  3289.3 65.0 %reduce-scatter.106.cloned.1.call-done = bf16[128,512]{1,0:T(8,128)(2,1)} async-done(((bf16[1024,512]{1,0:T(8,128)(2,1)}), bf16[128,512]{1,0:T(8,128)(2,1)}) %reduce-scatter.106.cloned.1.call-update) | async-done | bytes 131088
  3355.3 65.3 %reduce-scatter.108.cloned.1.call-done = bf16[128,512]{1,0:T(8,128)(2,1)} async-done(((bf16[1024,512]{1,0:T(8,128)(2,1)}), bf16[128,512]{1,0:T(8,128)(2,1)}) %reduce-scatter.108.cloned.1.call-update) | async-done | bytes 131088
  3421.7 65.0 %reduce-scatter.110.cloned.1.call-done = bf16[128,512]{1,0:T(8,128)(2,1)} async-done(((bf16[1024,512]{1,0:T(8,128)(2,1)}), bf16[128,512]{1,0:T(8,128)(2,1)}) %reduce-scatter.110.cloned.1.call-update) | async-done | bytes 131088
  3495.0 55.8 %reduce-scatter.56.cloned.1.call-done = bf16[128,128]{1,0:T(8,128)(2,1)} async-done(((bf16[1024,128]{1,0:T(8,128)(2,1)}), bf16[128,128]{1,0:T(8,128)(2,1)}) %reduce-scatter.56.cloned.1.call-update) | async-done | bytes 32784 | tf_op jit(solution)/shard_map/reduce_scatter | solution.py:433
  3552.1 62.6 %reduce-scatter.58.cloned.1.call-done = bf16[128,128]{1,0:T(8,128)(2,1)} async-done(((bf16[1024,128]{1,0:T(8,128)(2,1)}), bf16[128,128]{1,0:T(8,128)(2,1)}) %reduce-scatter.58.cloned.1.call-update) | async-done | bytes 32784 | tf_op jit(solution)/shard_map/reduce_scatter | solution.py:436
  3616.1 63.4 %reduce-scatter.94.cloned.1.call-done = bf16[128,256]{1,0:T(8,128)(2,1)} async-done(((bf16[1024,256]{1,0:T(8,128)(2,1)}), bf16[128,256]{1,0:T(8,128)(2,1)}) %reduce-scatter.94.cloned.1.call-update) | async-done | bytes 65552
  3681.2 62.6 %reduce-scatter.54.cloned.1.call-done = bf16[128,256]{1,0:T(8,128)(2,1)} async-done(((bf16[1024,256]{1,0:T(8,128)(2,1)}), bf16[128,256]{1,0:T(8,128)(2,1)}) %reduce-scatter.54.cloned.1.call-update) | async-done | bytes 65552 | tf_op jit(solution)/shard_map/reduce_scatter | solution.py:430
  3745.3 44.7 %reduce-scatter.52.cloned.1.call-done = bf16[512,1024]{1,0:T(8,128)(2,1)} async-done(((bf16[2048,1024]{1,0:T(8,128)(2,1)}), bf16[512,1024]{1,0:T(8,128)(2,1)}) %reduce-scatter.52.cloned.1.call-update) | async-done | bytes 1048592 | tf_op jit(solution)/shard_map/reduce_scatter | solution.py:418
  3792.0 39.5 %all-reduce.6 = (f32[1024]{0:T(1024)S(1)}, f32[1024]{0:T(1024)S(1)}) all-reduce(f32[1024]{0:T(1024)S(1)} %get-tuple-element.208, f32[1024]{0:T(1024)S(1)} %copy-done.133), channel_id=28, replica_groups=mesh['dp'=8,'tensor'=4] {'dp','tensor'}, use_global_device_ids=true, to_apply=%region_33.34.clone | all-reduce | flops 2048 | bytes 16384
  3837.3 89.2 %reduce-scatter.60.cloned.1.call-done = f32[32,32]{1,0:T(8,128)} async-done(((f32[1024,32]{1,0:T(8,128)}), f32[32,32]{1,0:T(8,128)}) %reduce-scatter.60.cloned.1.call-update) | async-done | bytes 4112 | tf_op jit(solution)/shard_map/reduce_scatter | solution.py:446
  (870 shorter events, 1241.6 us)
Async XLA Ops:
  265.3 282.9 %all-gather.69.cloned.1.call-start = ((), (), s32[]{:S(2)}) async-start(), calls=%async_computation.66 | async-start | bytes 1179648 | tf_op jit(solution)/shard_map/all_gather | solution.py:190
  265.9 324.1 %all-gather.73.cloned.1.call-start = ((), (), s32[]{:S(2)}) async-start(), calls=%async_computation.68 | async-start | bytes 1179648 | tf_op jit(solution)/shard_map/all_gather | solution.py:189
  266.4 364.7 %all-gather.75.cloned.1.call-start = ((), (), s32[]{:S(2)}) async-start(), calls=%async_computation.69 | async-start | bytes 1179648 | tf_op jit(solution)/shard_map/all_gather | solution.py:190
  267.0 406.0 %all-gather.79.cloned.1.call-start = ((), (), s32[]{:S(2)}) async-start(), calls=%async_computation.71 | async-start | bytes 1179648 | tf_op jit(solution)/shard_map/all_gather | solution.py:189
  267.8 446.4 %all-gather.81.cloned.1.call-start = ((), (), s32[]{:S(2)}) async-start(), calls=%async_computation.72 | async-start | bytes 1179648 | tf_op jit(solution)/shard_map/all_gather | solution.py:190
  268.4 487.7 %all-gather.85.cloned.1.call-start = ((), (), s32[]{:S(2)}) async-start(), calls=%async_computation.74 | async-start | bytes 1179648 | tf_op jit(solution)/shard_map/all_gather | solution.py:189
  269.1 528.2 %all-gather.87.cloned.1.call-start = ((), (), s32[]{:S(2)}) async-start(), calls=%async_computation.75 | async-start | bytes 1179648 | tf_op jit(solution)/shard_map/all_gather | solution.py:190
  269.7 567.9 %all-gather.65.cloned.1.call-start = ((), (), s32[]{:S(2)}) async-start(), calls=%async_computation.64 | async-start | bytes 1179648 | tf_op jit(solution)/shard_map/all_gather | solution.py:191
  270.4 608.0 %all-gather.71.cloned.1.call-start = ((), (), s32[]{:S(2)}) async-start(), calls=%async_computation.67 | async-start | bytes 1179648 | tf_op jit(solution)/shard_map/all_gather | solution.py:191
  271.2 648.0 %all-gather.77.cloned.1.call-start = ((), (), s32[]{:S(2)}) async-start(), calls=%async_computation.70 | async-start | bytes 1179648 | tf_op jit(solution)/shard_map/all_gather | solution.py:191
  271.9 688.1 %all-gather.83.cloned.1.call-start = ((), (), s32[]{:S(2)}) async-start(), calls=%async_computation.73 | async-start | bytes 1179648 | tf_op jit(solution)/shard_map/all_gather | solution.py:191
  272.7 728.2 %all-gather.89.cloned.1.call-start = ((), (), s32[]{:S(2)}) async-start(), calls=%async_computation.76 | async-start | bytes 1179648 | tf_op jit(solution)/shard_map/all_gather | solution.py:191
  273.4 769.1 %all-gather.91.cloned.1.call-start = ((), (), s32[]{:S(2)}) async-start(), calls=%async_computation.77 | async-start | bytes 1179648 | tf_op jit(solution)/shard_map/all_gather | solution.py:189
  274.0 809.8 %all-gather.93.cloned.1.call-start = ((), (), s32[]{:S(2)}) async-start(), calls=%async_computation.78 | async-start | bytes 1179648 | tf_op jit(solution)/shard_map/all_gather | solution.py:190
  353.7 770.3 %all-gather.95.cloned.1.call-start = ((), (), s32[]{:S(2)}) async-start(), calls=%async_computation.79 | async-start | bytes 1179648 | tf_op jit(solution)/shard_map/all_gather | solution.py:191
  354.3 811.9 %all-gather.97.cloned.1.call-start = ((), (), s32[]{:S(2)}) async-start(), calls=%async_computation.80 | async-start | bytes 1179648 | tf_op jit(solution)/shard_map/all_gather | solution.py:189
  354.9 852.5 %all-gather.99.cloned.1.call-start = ((), (), s32[]{:S(2)}) async-start(), calls=%async_computation.81 | async-start | bytes 1179648 | tf_op jit(solution)/shard_map/all_gather | solution.py:190
  355.5 892.2 %all-gather.101.cloned.1.call-start = ((), (), s32[]{:S(2)}) async-start(), calls=%async_computation.82 | async-start | bytes 1179648 | tf_op jit(solution)/shard_map/all_gather | solution.py:191
  1901.8 422.4 %reduce-scatter.62.cloned.1.call-start = ((), (), s32[]{:S(2)}) async-start(), calls=%async_computation.43 | async-start | bytes 1179648 | tf_op jit(solution)/shard_map/reduce_scatter | solution.py:353
  1905.1 420.0 %reduce-scatter.64.cloned.1.call-start = ((), (), s32[]{:S(2)}) async-start(), calls=%async_computation.44 | async-start | bytes 1179648 | tf_op jit(solution)/shard_map/reduce_scatter | solution.py:353
  1907.2 418.9 %reduce-scatter.66.cloned.1.call-start = ((), (), s32[]{:S(2)}) async-start(), calls=%async_computation.45 | async-start | bytes 1179648 | tf_op jit(solution)/shard_map/reduce_scatter | solution.py:353
  1909.3 417.7 %reduce-scatter.68.cloned.1.call-start = ((), (), s32[]{:S(2)}) async-start(), calls=%async_computation.46 | async-start | bytes 1179648 | tf_op jit(solution)/shard_map/reduce_scatter | solution.py:353
  1911.8 416.2 %reduce-scatter.70.cloned.1.call-start = ((), (), s32[]{:S(2)}) async-start(), calls=%async_computation.47 | async-start | bytes 1179648 | tf_op jit(solution)/shard_map/reduce_scatter | solution.py:353
  1915.1 413.9 %reduce-scatter.72.cloned.1.call-start = ((), (), s32[]{:S(2)}) async-start(), calls=%async_computation.48 | async-start | bytes 1179648 | tf_op jit(solution)/shard_map/reduce_scatter | solution.py:353
  1918.4 444.4 %reduce-scatter.74.cloned.1.call-start = ((), (), s32[]{:S(2)}) async-start(), calls=%async_computation.49 | async-start | bytes 1179648 | tf_op jit(solution)/shard_map/reduce_scatter | solution.py:353
  1921.6 507.0 %reduce-scatter.76.cloned.1.call-start = ((), (), s32[]{:S(2)}) async-start(), calls=%async_computation.50 | async-start | bytes 1179648 | tf_op jit(solution)/shard_map/reduce_scatter | solution.py:353
  1924.8 570.3 %reduce-scatter.78.cloned.1.call-start = ((), (), s32[]{:S(2)}) async-start(), calls=%async_computation.51 | async-start | bytes 1179648 | tf_op jit(solution)/shard_map/reduce_scatter | solution.py:356
  1928.2 632.6 %reduce-scatter.80.cloned.1.call-start = ((), (), s32[]{:S(2)}) async-start(), calls=%async_computation.52 | async-start | bytes 1179648 | tf_op jit(solution)/shard_map/reduce_scatter | solution.py:356
  1931.8 695.3 %reduce-scatter.82.cloned.1.call-start = ((), (), s32[]{:S(2)}) async-start(), calls=%async_computation.53 | async-start | bytes 1179648 | tf_op jit(solution)/shard_map/reduce_scatter | solution.py:356
  1935.3 757.8 %reduce-scatter.84.cloned.1.call-start = ((), (), s32[]{:S(2)}) async-start(), calls=%async_computation.54 | async-start | bytes 1179648 | tf_op jit(solution)/shard_map/reduce_scatter | solution.py:356
  1938.9 820.6 %reduce-scatter.86.cloned.1.call-start = ((), (), s32[]{:S(2)}) async-start(), calls=%async_computation.55 | async-start | bytes 1179648 | tf_op jit(solution)/shard_map/reduce_scatter | solution.py:356
  1942.3 883.0 %reduce-scatter.88.cloned.1.call-start = ((), (), s32[]{:S(2)}) async-start(), calls=%async_computation.56 | async-start | bytes 1179648 | tf_op jit(solution)/shard_map/reduce_scatter | solution.py:356
  1945.5 946.3 %reduce-scatter.90.cloned.1.call-start = ((), (), s32[]{:S(2)}) async-start(), calls=%async_computation.57 | async-start | bytes 1179648 | tf_op jit(solution)/shard_map/reduce_scatter | solution.py:356
  1948.7 1008.9 %reduce-scatter.92.cloned.1.call-start = ((), (), s32[]{:S(2)}) async-start(), calls=%async_computation.58 | async-start | bytes 1179648 | tf_op jit(solution)/shard_map/reduce_scatter | solution.py:356
  1950.8 1073.0 %reduce-scatter.96.cloned.1.call-start = ((), (), s32[]{:S(2)}) async-start(), calls=%async_computation.84 | async-start | bytes 1179648
  1954.3 1135.5 %reduce-scatter.98.cloned.1.call-start = ((), (), s32[]{:S(2)}) async-start(), calls=%async_computation.85 | async-start | bytes 1179648
  1957.8 1198.3 %reduce-scatter.100.cloned.1.call-start = ((), (), s32[]{:S(2)}) async-start(), calls=%async_computation.86 | async-start | bytes 1179648
  1960.6 1261.3 %reduce-scatter.102.cloned.1.call-start = ((), (), s32[]{:S(2)}) async-start(), calls=%async_computation.87 | async-start | bytes 1179648
  1963.5 1324.8 %reduce-scatter.104.cloned.1.call-start = ((), (), s32[]{:S(2)}) async-start(), calls=%async_computation.88 | async-start | bytes 1179648
  1966.2 1388.1 %reduce-scatter.106.cloned.1.call-start = ((), (), s32[]{:S(2)}) async-start(), calls=%async_computation.89 | async-start | bytes 1179648
  1969.0 1451.6 %reduce-scatter.108.cloned.1.call-start = ((), (), s32[]{:S(2)}) async-start(), calls=%async_computation.90 | async-start | bytes 1179648
  1971.8 1514.8 %reduce-scatter.110.cloned.1.call-start = ((), (), s32[]{:S(2)}) async-start(), calls=%async_computation.91 | async-start | bytes 1179648
  1974.6 1576.1 %reduce-scatter.56.cloned.1.call-start = ((), (), s32[]{:S(2)}) async-start(), calls=%async_computation.40 | async-start | bytes 294912 | tf_op jit(solution)/shard_map/reduce_scatter | solution.py:433
  2276.9 1337.8 %reduce-scatter.58.cloned.1.call-start = ((), (), s32[]{:S(2)}) async-start(), calls=%async_computation.41 | async-start | bytes 294912 | tf_op jit(solution)/shard_map/reduce_scatter | solution.py:436
  2281.4 1398.2 %reduce-scatter.94.cloned.1.call-start = ((), (), s32[]{:S(2)}) async-start(), calls=%async_computation.83 | async-start | bytes 589824
  2291.8 1452.0 %reduce-scatter.54.cloned.1.call-start = ((), (), s32[]{:S(2)}) async-start(), calls=%async_computation.39 | async-start | bytes 589824 | tf_op jit(solution)/shard_map/reduce_scatter | solution.py:430
  2302.0 1487.9 %reduce-scatter.52.cloned.1.call-start = ((), (), s32[]{:S(2)}) async-start(), calls=%async_computation.38 | async-start | bytes 5242880 | tf_op jit(solution)/shard_map/reduce_scatter | solution.py:418
  2309.1 1617.4 %reduce-scatter.60.cloned.1.call-start = ((), (), s32[]{:S(2)}) async-start(), calls=%async_computation.42 | async-start | bytes 540672 | tf_op jit(solution)/shard_map/reduce_scatter | solution.py:446
  (215 other events, 9182.7 us)
Sparse Core Ops, SparseCore 0:
  56.1 34.2 all-gather.50
  258.7 70.4 reduce-scatter.49
  1901.9 30.5 all-gather.52
Sparse Core Ops, SparseCore 1:
  261.5 39.1 all-gather.54
  302.9 38.9 all-gather.56
  384.4 39.4 all-gather.60
  426.2 38.9 all-gather.62
  468.1 38.9 all-gather.66
  509.3 38.9 all-gather.68
  551.0 38.9 all-gather.72
  592.2 38.9 all-gather.74
  634.1 38.9 all-gather.78
  675.2 38.9 all-gather.80
  717.1 38.9 all-gather.84
  758.3 38.9 all-gather.86
  880.7 38.5 all-gather.76
  962.3 38.5 all-gather.88
  1003.1 39.4 all-gather.90
  1044.9 38.9 all-gather.92
  1126.8 39.4 all-gather.96
  1168.5 38.9 all-gather.98
  1906.1 59.6 reduce-scatter.61
  1969.2 62.5 reduce-scatter.63
  2035.6 62.5 reduce-scatter.65
  2101.5 62.6 reduce-scatter.67
  2167.7 62.5 reduce-scatter.69
  2233.7 62.8 reduce-scatter.71
  2300.2 62.5 reduce-scatter.73
  2366.1 62.5 reduce-scatter.75
  2432.5 62.5 reduce-scatter.77
  2498.3 62.5 reduce-scatter.79
  2564.5 62.5 reduce-scatter.81
  2630.6 62.5 reduce-scatter.83
  2696.9 62.5 reduce-scatter.85
  2762.8 62.5 reduce-scatter.87
  2829.2 62.5 reduce-scatter.89
  2895.0 62.5 reduce-scatter.91
  2961.3 62.5 reduce-scatter.95
  3027.1 62.6 reduce-scatter.97
  3093.5 62.5 reduce-scatter.99
  3159.4 62.5 reduce-scatter.101
  3225.7 62.5 reduce-scatter.103
  3291.7 62.5 reduce-scatter.105
  3358.1 62.5 reduce-scatter.107
  3424.1 62.5 reduce-scatter.109
  3490.3 60.4 reduce-scatter.55
  3554.3 60.4 reduce-scatter.57
  3618.5 61.0 reduce-scatter.93
  3682.8 61.0 reduce-scatter.53
  3746.5 43.4 reduce-scatter.51
  3792.7 133.8 reduce-scatter.59
  (6 shorter events, 229.0 us)
where the time goes:
time: 3950 us; the launch traced here: 3930 us
  waiting for transfers between devices  2460 us (62%)
  blocking collectives  444 us (11%)
  matrix products  427 us (11%)
  local copies, waits for them, and re-layouts  395 us (10%)
  other arithmetic  150 us (4%)
    unnamed x66, waiting for transfers between devices  596 us
    reduce_scatter x8, waiting for transfers between devices, per_device(): lax.psum_scatter(up_w_grad.astype(jnp.bfloat16), 'dp', scatter_dimension=...  520 us
    all_gather x8, waiting for transfers between devices, fetch_expert(): lax.all_gather(down_part, 'dp', axis=1, tiled=True)  261 us
    all_gather x8, waiting for transfers between devices, fetch_expert(): lax.all_gather(up_part, 'dp', axis=0, tiled=True)  228 us
    all_gather x8, waiting for transfers between devices, fetch_expert(): lax.all_gather(gate_part, 'dp', axis=0, tiled=True)  214 us
    all_gather x1, blocking collectives, per_device(): lax.all_gather(w_router, ('dp', 'tensor'), axis=0, tiled=True)  134 us
    all_to_all x1, blocking collectives, to_owner(): lax.all_to_all(outgoing, 'tensor', split_axis=0, concat_axis=2, tiled=True)  109 us
    all_to_all x2, waiting for transfers between devices, to_source(): lax.all_to_all(stacked[None], 'tensor', split_axis=2, concat_axis=0, tile...  104 us
  transfers between devices with their start and end apart: 60, of which 46 were waited for; matrix products, arithmetic and copies ran while one was open for 15% of the time, Pallas kernels for 0%

commit v1 on v0

v1 whole, which is shorter than its diff:
```python
import functools
import math

import jax
import jax.numpy as jnp
from jax import lax
from jax.experimental import pallas as pl
from jax.experimental.pallas import tpu as pltpu
from jax.sharding import PartitionSpec as P

HEAD_DIM = 64
E = 32
TOPK = 8
SEQUENCE_LENGTH = 2048


HIGHEST = lax.Precision.HIGHEST
EPSILON = 1e-06
ROTARY_BASE = 10000.0
MASKED_SCORE = -1e30
BLOCK = 512
F32 = jnp.float32
BF16 = jnp.bfloat16


def rms_forward(values, gain):
    factor = lax.rsqrt(jnp.mean(values * values, axis=-1, keepdims=True) + EPSILON)
    return (values * factor * gain, factor)


def rms_backward(values, factor, gain, grad):
    normal = values * factor
    gain_grad = jnp.sum(grad * normal, axis=0)
    inner = grad * gain
    back = factor * (inner - normal * jnp.mean(inner * normal, axis=-1, keepdims=True))
    return (back, gain_grad)


def positions_of(segment_rows):
    length = segment_rows.shape[1]
    place = jnp.arange(length, dtype=jnp.int32)
    shifted = jnp.concatenate([segment_rows[:, :1], segment_rows[:, :-1]], axis=1)
    opening = (place[None, :] == 0) | (segment_rows != shifted)
    begin = lax.cummax(jnp.where(opening, place[None, :], 0), axis=1)
    return place[None, :] - begin


def rotary_tables(position, head_size):
    half_size = head_size // 2
    frequency = jnp.exp(
        jnp.arange(half_size, dtype=jnp.float32) * (-2.0 * math.log(ROTARY_BASE) / head_size)
    )
    angle = position.astype(jnp.float32)[:, None] * frequency[None, :]
    return (jnp.cos(angle), jnp.sin(angle))


def turn_heads(values, cosine_table, sine_values):
    half_size = values.shape[-1] // 2
    front_half = values[..., :half_size]
    back_half = values[..., half_size:]
    cos_b = cosine_table[None]
    sin_b = sine_values[None]
    return jnp.concatenate(
        [front_half * cos_b - back_half * sin_b, back_half * cos_b + front_half * sin_b], axis=-1
    )


def to_heads(values, heads):
    return values.reshape(values.shape[0], heads, HEAD_DIM).transpose(1, 0, 2)


def from_heads(values):
    return values.transpose(1, 0, 2).reshape(values.shape[1], -1)


def dot_nt(left, right):
    return lax.dot_general(left, right, (((1,), (1,)), ((), ())), preferred_element_type=F32)


def dot_tn(left, right):
    return lax.dot_general(left, right, (((0,), (0,)), ((), ())), preferred_element_type=F32)


def allowed_block(query_segments, key_segments, i, j, block):
    row = i * block + lax.broadcasted_iota(jnp.int32, (block, block), 0)
    column = j * block + lax.broadcasted_iota(jnp.int32, (block, block), 1)
    return (query_segments == key_segments) & (column <= row)


def attend_kernel(block, scale, q_ref, k_ref, v_ref, segq_ref, segk_ref, out_ref, total_ref):
    i = pl.program_id(1)
    queries = q_ref[0]
    query_segments = segq_ref[...]

    def step(j, carry):
        row_max, row_sum, mix = carry
        start = pl.multiple_of(j * block, block)
        scores = dot_nt(queries, k_ref[0, pl.ds(start, block), :]) * scale
        allowed = allowed_block(query_segments, segk_ref[j], i, j, block)
        scores = jnp.where(allowed, scores, MASKED_SCORE)
        new_max = jnp.maximum(row_max, jnp.max(scores, axis=-1, keepdims=True))
        weights = jnp.exp(scores - new_max)
        shrink = jnp.exp(row_max - new_max)
        row_sum = row_sum * shrink + jnp.sum(weights, axis=-1, keepdims=True)
        mix = mix * shrink + jnp.dot(
            weights.astype(BF16), v_ref[0, pl.ds(start, block), :], preferred_element_type=F32
        )
        return new_max, row_sum, mix

    row_max, row_sum, mix = lax.fori_loop(
        0,
        i + 1,
        step,
        (
            jnp.full((block, 1), MASKED_SCORE, F32),
            jnp.zeros((block, 1), F32),
            jnp.zeros((block, HEAD_DIM), F32),
        ),
    )
    out_ref[0] = (mix / row_sum).astype(BF16)
    total_ref[0] = row_max + jnp.log(row_sum)


def attend_forward(queries, keys, values, segments, scale):
    heads, length, _ = queries.shape
    share = heads // keys.shape[0]
    block = min(BLOCK, length)
    blocks = length // block
    return pl.pallas_call(
        functools.partial(attend_kernel, block, scale),
        grid=(heads, blocks),
        in_specs=[
            pl.BlockSpec((1, block, HEAD_DIM), lambda h, i: (h, i, 0)),
            pl.BlockSpec((1, length, HEAD_DIM), lambda h, i: (h // share, 0, 0)),
            pl.BlockSpec((1, length, HEAD_DIM), lambda h, i: (h // share, 0, 0)),
            pl.BlockSpec((block, 1), lambda h, i: (i, 0)),
            pl.BlockSpec((blocks, 1, block), lambda h, i: (0, 0, 0)),
        ],
        out_specs=[
            pl.BlockSpec((1, block, HEAD_DIM), lambda h, i: (h, i, 0)),
            pl.BlockSpec((1, block, 1), lambda h, i: (h, i, 0)),
        ],
        out_shape=[
            jax.ShapeDtypeStruct((heads, length, HEAD_DIM), BF16),
            jax.ShapeDtypeStruct((heads, length, 1), F32),
        ],
        compiler_params=pltpu.CompilerParams(vmem_limit_bytes=32 * 1024 * 1024),
        cost_estimate=pl.CostEstimate(
            flops=heads * length * length * HEAD_DIM * 3,
            bytes_accessed=heads * length * HEAD_DIM * 8,
            transcendentals=heads * length * length // 2,
        ),
    )(queries, keys, values, segments.reshape(length, 1), segments.reshape(blocks, 1, block))


def attend_back_kernel(
    block,
    scale,
    q_ref,
    k_ref,
    v_ref,
    grad_ref,
    mix_ref,
    total_ref,
    segq_ref,
    segk_ref,
    dq_ref,
    dk_ref,
    dv_ref,
):
    g = pl.program_id(1)
    i = pl.program_id(2)

    @pl.when((g == 0) & (i == 0))
    def _():
        dk_ref[...] = jnp.zeros_like(dk_ref)
        dv_ref[...] = jnp.zeros_like(dv_ref)

    queries = q_ref[0]
    grad = grad_ref[0]
    total = total_ref[0]
    query_segments = segq_ref[...]
    inner = jnp.sum(grad.astype(F32) * mix_ref[0].astype(F32), axis=-1, keepdims=True)

    def step(j, query_grad):
        start = pl.multiple_of(j * block, block)
        here = pl.ds(start, block)
        keys = k_ref[0, here, :]
        scores = dot_nt(queries, keys) * scale
        allowed = allowed_block(query_segments, segk_ref[j], i, j, block)
        softmaxed = jnp.exp(jnp.where(allowed, scores - total, MASKED_SCORE))
        prob_grad = dot_nt(grad, v_ref[0, here, :])
        score_grad = (softmaxed * (prob_grad - inner)).astype(BF16)
        dv_ref[0, here, :] += dot_tn(softmaxed.astype(BF16), grad)
        dk_ref[0, here, :] += dot_tn(score_grad, queries) * scale
        return query_grad + jnp.dot(score_grad, keys, preferred_element_type=F32)

    query_grad = lax.fori_loop(0, i + 1, step, jnp.zeros((block, HEAD_DIM), F32))
    dq_ref[0] = query_grad * scale


def attend_backward(queries, keys, values, segments, totals, mix, mix_grad, scale):
    heads, length, _ = queries.shape
    kv_heads = keys.shape[0]
    share = heads // kv_heads
    block = min(BLOCK, length)
    blocks = length // block
    by_query = pl.BlockSpec((1, block, HEAD_DIM), lambda c, g, i: (c * share + g, i, 0))
    by_key = pl.BlockSpec((1, length, HEAD_DIM), lambda c, g, i: (c, 0, 0))
    return pl.pallas_call(
        functools.partial(attend_back_kernel, block, scale),
        grid=(kv_heads, share, blocks),
        in_specs=[
            by_query,
            by_key,
            by_key,
            by_query,
            by_query,
            pl.BlockSpec((1, block, 1), lambda c, g, i: (c * share + g, i, 0)),
            pl.BlockSpec((block, 1), lambda c, g, i: (i, 0)),
            pl.BlockSpec((blocks, 1, block), lambda c, g, i: (0, 0, 0)),
        ],
        out_specs=[by_query, by_key, by_key],
        out_shape=[
            jax.ShapeDtypeStruct((heads, length, HEAD_DIM), F32),
            jax.ShapeDtypeStruct((kv_heads, length, HEAD_DIM), F32),
            jax.ShapeDtypeStruct((kv_heads, length, HEAD_DIM), F32),
        ],
        compiler_params=pltpu.CompilerParams(vmem_limit_bytes=32 * 1024 * 1024),
        cost_estimate=pl.CostEstimate(
            flops=heads * length * length * HEAD_DIM * 6,
            bytes_accessed=heads * length * HEAD_DIM * 24,
            transcendentals=heads * length * length // 2,
        ),
    )(
        queries,
        keys,
        values,
        mix_grad,
        mix,
        totals,
        segments.reshape(length, 1),
        segments.reshape(blocks, 1, block),
    )


def per_device(
    tokens,
    cotangent,
    segments,
    routes,
    gain_attn,
    w_query,
    key_weight,
    value_weight,
    w_out,
    gain_moe,
    w_router,
    w_gate,
    w_up,
    w_down,
):
    groups = lax.axis_size("tensor")
    copies = lax.axis_size("dp")
    member = lax.axis_index("tensor")
    row_total, width = tokens.shape
    length = segments.shape[0]
    scale = HEAD_DIM ** (-0.5)
    local_experts, part, hidden_units = w_gate.shape
    capacity = max(2, row_total * TOPK * 9 // (8 * E))
    gain_part = gain_attn.shape[0]
    q_width = w_query.shape[1]
    kv_width = key_weight.shape[1]
    q_heads = q_width // HEAD_DIM
    kv_heads = kv_width // HEAD_DIM

    route_size = row_total * TOPK
    out_size = w_out.size
    small_size = gain_part * (E + 2)
    extra = jnp.concatenate(
        [
            routes.astype(BF16).reshape(-1),
            w_out.T.reshape(-1),
            w_router.reshape(-1),
            gain_attn,
            gain_moe,
        ]
    )
    extra_rows = -(-extra.size // (16 * width)) * 16
    extra = jnp.pad(extra, (0, extra_rows * width - extra.size)).reshape(extra_rows, width)
    first = lax.all_gather(jnp.concatenate([tokens, cotangent, extra], axis=0), "tensor", axis=0)
    all_tokens = first[:, :row_total].reshape(length, width)
    all_cotangent = first[:, row_total : 2 * row_total].reshape(length, width)
    extras = first[:, 2 * row_total :].reshape(groups, extra_rows * width)
    all_routes = extras[:, :route_size].reshape(length, TOPK).astype(jnp.int32)
    out_block = extras[:, route_size : route_size + out_size].reshape(groups, part, q_width)
    out_block = out_block.transpose(1, 0, 2).reshape(part, groups * q_width)
    small = extras[:, route_size + out_size : route_size + out_size + small_size].reshape(-1)

    block = jnp.concatenate([w_query, key_weight, value_weight, out_block], axis=1)
    small_rows = -(-small.size // (16 * block.shape[1])) * 16
    small_block = jnp.pad(small, (0, small_rows * block.shape[1] - small.size))
    second = lax.all_gather(
        jnp.concatenate([block, small_block.reshape(small_rows, -1)], axis=0), "dp", axis=0
    )
    weights = second[:, :part].reshape(width, block.shape[1])
    qkv_width = q_width + 2 * kv_width
    qkv_w = weights[:, :qkv_width]
    out_w_t = weights[:, qkv_width:]
    smalls = second[:, part:].reshape(copies, -1)[:, : small.size].reshape(-1, small_size)
    router = smalls[:, : gain_part * E].reshape(width, E)
    gain_a = smalls[:, gain_part * E : gain_part * (E + 1)].reshape(width).astype(F32)
    gain_m = smalls[:, gain_part * (E + 1) :].reshape(width).astype(F32)

    gate_part, up_part, down_part, second = lax.optimization_barrier(
        (w_gate, w_up, w_down.transpose(0, 2, 1), second)
    )
    gate_w = lax.all_gather(gate_part, "dp", axis=1, tiled=True)
    up_w = lax.all_gather(up_part, "dp", axis=1, tiled=True)
    down_w = lax.all_gather(down_part, "dp", axis=1, tiled=True)

    inputs = all_tokens.astype(F32)
    normed, factor_a = rms_forward(inputs, gain_a)
    normed = normed.astype(BF16)
    cosine_table, sine_values = rotary_tables(
        positions_of(segments.reshape(-1, SEQUENCE_LENGTH)).reshape(length), HEAD_DIM
    )
    linear = jnp.dot(normed, qkv_w, preferred_element_type=F32)
    queries = turn_heads(to_heads(linear[:, :q_width], q_heads), cosine_table, sine_values)
    queries = queries.astype(BF16)
    keys = turn_heads(
        to_heads(linear[:, q_width : q_width + kv_width], kv_heads), cosine_table, sine_values
    ).astype(BF16)
    values = to_heads(linear[:, q_width + kv_width :].astype(BF16), kv_heads)
    mix_heads, totals = attend_forward(queries, keys, values, segments, scale)
    mixed = from_heads(mix_heads)
    all_mixed = lax.all_gather(mixed, "tensor", axis=1, tiled=True)
    hidden = inputs + dot_nt(all_mixed, out_w_t)
    normed_moe, factor_m = rms_forward(hidden, gain_m)
    low_moe = normed_moe.astype(BF16)

    logits = jnp.dot(low_moe, router, preferred_element_type=F32)
    expert_ids = jnp.arange(E, dtype=jnp.int32)
    chosen = jnp.any(all_routes[:, :, None] == expert_ids[None, None, :], axis=1)
    peak = jnp.max(jnp.where(chosen, logits, MASKED_SCORE), axis=-1, keepdims=True)
    powers = jnp.where(chosen, jnp.exp(jnp.where(chosen, logits - peak, 0.0)), 0.0)
    gates = powers / jnp.sum(powers, axis=-1, keepdims=True)

    first_expert = member * local_experts
    mine = lax.dynamic_slice_in_dim(chosen, first_expert, local_experts, 1)
    mine = mine.reshape(groups, row_total, local_experts)
    my_gates = lax.dynamic_slice_in_dim(gates, first_expert, local_experts, 1)
    my_gates = my_gates.reshape(groups, row_total, local_experts).transpose(0, 2, 1)
    lower = jnp.tril(jnp.ones((row_total, row_total), BF16))
    rank = jnp.einsum("tu,sue->set", lower, mine.astype(BF16), preferred_element_type=F32)
    place = jnp.where(mine.transpose(0, 2, 1), rank.astype(jnp.int32) - 1, -1)
    slots = jnp.arange(capacity, dtype=jnp.int32)
    named = place[:, :, None, :] == slots[None, None, :, None]
    slot_gate = jnp.sum(jnp.where(named, my_gates[:, :, None, :], 0.0), axis=-1)
    onehot = named.astype(BF16).reshape(groups, local_experts * capacity, row_total)
    slot_rows = groups * capacity

    def dispatch(rows):
        picked = jnp.einsum(
            "sct,std->scd",
            onehot,
            rows.reshape(groups, row_total, width),
            preferred_element_type=F32,
        ).astype(BF16)
        picked = picked.reshape(groups, local_experts, capacity, width)
        return picked.transpose(1, 0, 2, 3).reshape(local_experts, slot_rows, width)

    def combine(rows):
        rows = rows.reshape(local_experts, groups, capacity, width).transpose(1, 0, 2, 3)
        rows = rows.reshape(groups, local_experts * capacity, width)
        return jnp.einsum("sct,scd->std", onehot, rows, preferred_element_type=F32).reshape(
            length, width
        )

    received = dispatch(low_moe)
    grad_rows = dispatch(all_cotangent)
    gate_rows = slot_gate.transpose(1, 0, 2).reshape(local_experts, slot_rows, 1)
    pre_gate = jnp.einsum("erd,edf->erf", received, gate_w, preferred_element_type=F32)
    pre_up = jnp.einsum("erd,edf->erf", received, up_w, preferred_element_type=F32)
    sigmoid_gate = jax.nn.sigmoid(pre_gate)
    silu_gate = pre_gate * sigmoid_gate
    activation = (silu_gate * pre_up).astype(BF16)
    expert_out = jnp.einsum("erf,edf->erd", activation, down_w, preferred_element_type=F32)
    expert_out = expert_out.astype(BF16).astype(F32)
    slot_grad = jnp.sum(grad_rows.astype(F32) * expert_out, axis=-1)
    slot_grad = slot_grad.reshape(local_experts, groups, capacity).transpose(1, 0, 2)
    my_gate_grad = jnp.sum(jnp.where(named, slot_grad[:, :, :, None], 0.0), axis=2)
    my_gate_grad = my_gate_grad.transpose(0, 2, 1).reshape(length, local_experts)
    moe_part = combine((gate_rows * expert_out).astype(BF16)).astype(BF16)
    moe_own = lax.psum_scatter(moe_part, "tensor", scatter_dimension=0, tiled=True)
    own_start = member * row_total
    hidden_own = lax.dynamic_slice_in_dim(hidden, own_start, row_total, 0)
    mixed_out = (hidden_own + moe_own.astype(F32)).astype(BF16)

    out_grad = (gate_rows * grad_rows.astype(F32)).astype(BF16)
    act_grad = jnp.einsum("erd,edf->erf", out_grad, down_w, preferred_element_type=F32)
    gate_grad = (act_grad * pre_up * sigmoid_gate * (1.0 + pre_gate * (1.0 - sigmoid_gate))).astype(
        BF16
    )
    up_grad = (act_grad * silu_gate).astype(BF16)
    row_grad = jnp.einsum("erf,edf->erd", gate_grad, gate_w, preferred_element_type=F32)
    row_grad = row_grad + jnp.einsum("erf,edf->erd", up_grad, up_w, preferred_element_type=F32)
    norm_part = combine(row_grad.astype(BF16)).astype(BF16)
    placed_grad = lax.dynamic_update_slice_in_dim(
        jnp.zeros((length, E), F32), my_gate_grad, first_expert, 1
    )
    high = lax.reduce_precision(placed_grad, 8, 7)
    sides = jnp.concatenate(
        [high.astype(BF16), (placed_grad - high).astype(BF16), jnp.zeros((length, 64), BF16)],
        axis=1,
    )
    joined = jnp.concatenate([norm_part, sides], axis=1)
    joined, gate_grad, up_grad, activation, out_grad = lax.optimization_barrier(
        (joined, gate_grad, up_grad, activation, out_grad)
    )
    joined = lax.psum(joined, "tensor").astype(F32)
    gate_w_grad = jnp.einsum("erd,erf->edf", received, gate_grad, preferred_element_type=F32)
    gate_share = lax.psum_scatter(
        gate_w_grad.astype(BF16), "dp", scatter_dimension=1, tiled=True
    ).astype(F32)
    up_w_grad = jnp.einsum("erd,erf->edf", received, up_grad, preferred_element_type=F32)
    up_share = lax.psum_scatter(
        up_w_grad.astype(BF16), "dp", scatter_dimension=1, tiled=True
    ).astype(F32)
    down_w_grad = jnp.einsum("erd,erf->edf", out_grad, activation, preferred_element_type=F32)
    down_share = lax.psum_scatter(
        down_w_grad.astype(BF16), "dp", scatter_dimension=1, tiled=True
    ).astype(F32)
    down_share = down_share.transpose(0, 2, 1)

    all_gate_grad = joined[:, width : width + E] + joined[:, width + E : width + 2 * E]
    logit_grad = gates * (all_gate_grad - jnp.sum(gates * all_gate_grad, axis=-1, keepdims=True))
    norm_moe_grad = joined[:, :width] + jnp.dot(
        logit_grad, router.astype(F32).T, precision=HIGHEST
    )
    logit_high = lax.reduce_precision(logit_grad, 8, 7)
    logit_pair = jnp.concatenate(
        [logit_high.astype(BF16), (logit_grad - logit_high).astype(BF16)], axis=1
    )
    router_pair = dot_tn(low_moe, logit_pair)
    router_grad = router_pair[:, :E] + router_pair[:, E:]
    hidden_back, gain_m_grad = rms_backward(hidden, factor_m, gain_m, norm_moe_grad)
    hidden_grad = all_cotangent.astype(F32) + hidden_back
    branch_grad = hidden_grad.astype(BF16)
    hidden_grad_own = lax.dynamic_slice_in_dim(hidden_grad, own_start, row_total, 0)

    out_w_grad = dot_tn(branch_grad, mixed)
    my_out_w = lax.dynamic_slice_in_dim(out_w_t, member * q_width, q_width, 1)
    mix_grad = jnp.dot(branch_grad, my_out_w, preferred_element_type=F32).astype(BF16)
    query_grad, key_grad, value_grad = attend_backward(
        queries, keys, values, segments, totals, mix_heads, to_heads(mix_grad, q_heads), scale
    )
    linear_grad = jnp.concatenate(
        [
            from_heads(turn_heads(query_grad, cosine_table, -sine_values).astype(BF16)),
            from_heads(turn_heads(key_grad, cosine_table, -sine_values).astype(BF16)),
            from_heads(value_grad.astype(BF16)),
        ],
        axis=1,
    )
    qkv_w_grad = dot_tn(normed, linear_grad)
    summed = dot_nt(linear_grad, qkv_w)
    gain_a_grad = jnp.sum(summed * (inputs * factor_a), axis=0)
    side_grads = jnp.concatenate(
        [router_grad, gain_m_grad[:, None], gain_a_grad[:, None], jnp.zeros((width, 94), F32)],
        axis=1,
    )
    weight_grads = jnp.concatenate([qkv_w_grad, out_w_grad, side_grads], axis=1).astype(BF16)
    shares = lax.psum_scatter(weight_grads, "dp", scatter_dimension=0, tiled=True)
    side_start = qkv_width + q_width
    gain_a_block = shares[:, side_start + E + 1].reshape(groups, 1, gain_part)
    gain_a_block = jnp.pad(gain_a_block, ((0, 0), (0, 15), (0, width - gain_part)))
    summed = jnp.concatenate(
        [summed.astype(BF16).reshape(groups, row_total, width), gain_a_block], axis=1
    ).reshape(groups * (row_total + 16), width)
    reduced = lax.psum_scatter(summed, "tensor", scatter_dimension=0, tiled=True).astype(F32)
    gain_a_share = reduced[row_total, :gain_part]
    norm_attn_grad = reduced[:row_total]
    inputs_own = tokens.astype(F32)
    factor_own = lax.rsqrt(jnp.mean(inputs_own * inputs_own, axis=-1, keepdims=True) + EPSILON)
    input_back, _ = rms_backward(inputs_own, factor_own, gain_a, norm_attn_grad)
    input_grad = hidden_grad_own + input_back
    shares = shares.astype(F32)
    mine_small = lax.dynamic_slice_in_dim(
        shares[:, side_start : side_start + E + 1], member * gain_part, gain_part, 0
    )
    return (
        mixed_out,
        input_grad,
        gain_a_share,
        shares[:, :q_width],
        shares[:, q_width : q_width + kv_width],
        shares[:, q_width + kv_width : qkv_width],
        shares[:, qkv_width:side_start].T,
        mine_small[:, E],
        mine_small[:, :E],
        gate_share,
        up_share,
        down_share,
    )


def solution(mesh):
    placed = (
        P(("dp", "tensor"), None),
        P(("dp", "tensor"), None),
        P("dp"),
        P(("dp", "tensor"), None),
        P(("dp", "tensor")),
        P("dp", "tensor"),
        P("dp", "tensor"),
        P("dp", "tensor"),
        P("tensor", "dp"),
        P(("dp", "tensor")),
        P(("dp", "tensor"), None),
        P("tensor", "dp", None),
        P("tensor", "dp", None),
        P("tensor", None, "dp"),
    )
    return jax.shard_map(
        per_device,
        mesh=mesh,
        in_specs=placed,
        out_specs=(
            P(("dp", "tensor"), None),
            P(("dp", "tensor"), None),
            P(("dp", "tensor")),
            P("dp", "tensor"),
            P("dp", "tensor"),
            P("dp", "tensor"),
            P("tensor", "dp"),
            P(("dp", "tensor")),
            P(("dp", "tensor"), None),
            P("tensor", "dp", None),
            P("tensor", "dp", None),
            P("tensor", None, "dp"),
        ),
        check_vma=False,
    )
```

time: 3950 us -> 1620 us (0.41)
  waiting for transfers between devices: 2460 us -> 1000 us
  blocking collectives: 444 us -> 0 us
  local copies, waits for them, and re-layouts: 395 us -> 168 us
  matrix products: 427 us -> 225 us
  Pallas kernels: 0 us -> 88.8 us
    reduce_scatter x22 -> x4, waiting for transfers between devices: 960 us -> 439 us  [the longest x1 149 us: per_device(): lax.psum_scatter(gate_w_grad.astype(BF16), 'dp', scatter_dimension=1, til...]
    unnamed x66 -> x15, waiting for transfers between devices: 596 us -> 79 us
    all_gather x26 -> x6, waiting for transfers between devices: 703 us -> 407 us  [the longest x1 113 us: per_device(): up_w = lax.all_gather(up_part, 'dp', axis=1, tiled=True)]
    all_gather x5 -> x0, blocking collectives: 254 us -> none  [the longest x1 134 us: per_device(): lax.all_gather(w_router, ('dp', 'tensor'), axis=0, tiled=True)]
    all_to_all x3 -> x0, waiting for transfers between devices: 206 us -> none  [the longest x2 104 us: to_source(): lax.all_to_all(stacked[None], 'tensor', split_axis=2, concat_axis=0, tile...]
    dot_general x115 -> x23, matrix products: 427 us -> 225 us  [the longest x2 22.2 us: combine(): jnp.einsum('sct,scd->std', onehot, rows, preferred_element_type=F32)]
    all_to_all x1 -> x0, blocking collectives: 109 us -> none  [to_owner(): lax.all_to_all(outgoing, 'tensor', split_axis=0, concat_axis=2, tiled=True)]
    gather x4 -> x0, local copies, waits for them, and re-layouts: 92.3 us -> none  [the longest x1 26.1 us: per_device(): assigned = returned[slot_of].reshape(row_total, TOPK, model_width)]
  transfers between devices with their start and end apart: 60 -> 13, of which waited for: 46 -> 12; matrix products, arithmetic and copies ran while one was open for 15% -> 15% of each run, Pallas kernels for 0% -> 0%
where the time goes in v1:
time: 1620 us
  waiting for transfers between devices  1000 us (62%)
  matrix products  225 us (14%)
  local copies, waits for them, and re-layouts  168 us (10%)
  other arithmetic  119 us (7%)
  Pallas kernels  88.8 us (5%)
    reduce_scatter x1, waiting for transfers between devices, per_device(): lax.psum_scatter(gate_w_grad.astype(BF16), 'dp', scatter_dimension=1, til...  149 us
    reduce_scatter x1, waiting for transfers between devices, per_device(): lax.psum_scatter(up_w_grad.astype(BF16), 'dp', scatter_dimension=1, tiled...  148 us
    reduce_scatter x1, waiting for transfers between devices, per_device(): lax.psum_scatter(down_w_grad.astype(BF16), 'dp', scatter_dimension=1, til...  142 us
    all_gather x1, waiting for transfers between devices, per_device(): up_w = lax.all_gather(up_part, 'dp', axis=1, tiled=True)  113 us
    all_gather x1, waiting for transfers between devices, per_device(): down_w = lax.all_gather(down_part, 'dp', axis=1, tiled=True)  110 us
    all_gather x1, waiting for transfers between devices, per_device(): gate_w = lax.all_gather(gate_part, 'dp', axis=1, tiled=True)  82.8 us
    unnamed x15, waiting for transfers between devices  79 us
    psum x1, waiting for transfers between devices, per_device(): joined = lax.psum(joined, 'tensor').astype(F32)  74.6 us
  transfers between devices with their start and end apart: 13, of which 12 were waited for; matrix products, arithmetic and copies ran while one was open for 15% of the time, Pallas kernels for 0%

profile of v1, /device:TPU:0, one launch (start us, length us, event | category | flops | bytes accessed | tf_op | source)
XLA Modules:
  0.0 1616.0 jit_solution(18331454455401778250)
XLA Ops:
  15.2 62.9 %all-gather.17.cloned.1.call-done = bf16[4288,1024]{1,0:T(8,128)(2,1)} async-done(((bf16[1072,1024]{1,0:T(8,128)(2,1)}), bf16[4288,1024]{1,0:T(8,128)(2,1)}) %all-gather.17.cloned.1.call-update) | async-done | bytes 8781840 | tf_op jit(solution)/shard_map/all_gather | solution.py:291
  84.9 5.8 fusion.29
  90.8 7.9 fusion.52
  98.7 9.3 copy.366
  111.1 35.7 %all-gather.19.cloned.1.call-done = bf16[1152,1536]{1,0:T(8,128)(2,1)} async-done(((bf16[144,1536]{1,0:T(8,128)(2,1)}), bf16[1152,1536]{1,0:T(8,128)(2,1)}) %all-gather.19.cloned.1.call-update) | async-done | bytes 3538960 | tf_op jit(solution)/shard_map/all_gather | solution.py:303
  152.7 6.4 fusion.24
  180.1 38.3 %shard_map.229 = (bf16[4,2048,64]{2,1,0:T(8,128)(2,1)S(1)}, f32[4,2048,1]{2,1,0:T(8,128)S(1)}) custom-call(bf16[4,2048,64]{2,1,0:T(8,128)(2,1)S(1)} %pad_maximum_fusion.1.q_ref, bf16[2,2048,64]{2,1,0:T(8,128)(2,1)S(1)} %pad_maximum_fusion.3.k_ref, bf16[2,2048,64]{2,1,0:T(8,128)(2,1)S(1)} %bitcast.147, s32[2048,1]{1,0:T(8,128)S(1)} %copy-done.11, ...), custom_call_target="tpu_custom_call" | custom-call | flops 3221225472 | bytes 4194304 | tf_op jit(solution)/shard_map/pallas_call | solution.py:129
  229.6 10.5 convolution_convert_fusion
  240.1 12.9 copy.340
  255.7 8.2 multiply_reduce_fusion.3
  270.5 6.6 copy.367
  277.0 9.8 convolution_convert_fusion.1
  286.8 9.2 copy.334
  299.9 82.8 %all-gather.11.cloned.1.call-done = bf16[8,1024,512]{2,1,0:T(8,128)(2,1)} async-done(((bf16[8,128,512]{2,1,0:T(8,128)(2,1)}), bf16[8,1024,512]{2,1,0:T(8,128)(2,1)}) %all-gather.11.cloned.1.call-update) | async-done | bytes 8388624 | tf_op jit(solution)/shard_map/all_gather | solution.py:318
  382.7 12.3 fusion.55
  395.0 112.8 %all-gather.13.cloned.1.call-done = bf16[8,1024,512]{2,1,0:T(8,128)(2,1)} async-done(((bf16[8,128,512]{2,1,0:T(8,128)(2,1)}), bf16[8,1024,512]{2,1,0:T(8,128)(2,1)}) %all-gather.13.cloned.1.call-update) | async-done | bytes 8388624 | tf_op jit(solution)/shard_map/all_gather | solution.py:319
  507.8 15.4 multiply_convert_fusion.3
  523.2 110.4 %all-gather.15.cloned.1.call-done = bf16[8,1024,512]{2,1,0:T(8,128)(2,1)} async-done(((bf16[8,128,512]{2,1,0:T(8,128)(2,1)}), bf16[8,1024,512]{2,1,0:T(8,128)(2,1)}) %all-gather.15.cloned.1.call-update) | async-done | bytes 8388624 | tf_op jit(solution)/shard_map/all_gather | solution.py:320
  633.6 16.7 %fusion.1 = (f32[8,576]{1,0:T(8,128)S(1)}, bf16[8,576,1024]{2,1,0:T(8,128)(2,1)}) fusion(f32[8,576,1024]{2,1,0:T(8,128)} %bitcast.154, bf16[8,576,512]{2,1,0:T(8,128)(2,1)} %get-tuple-element.37, bf16[8,1024,512]{2,1,0:T(8,128)(2,1)} %all-gather.15.cloned.1.call-done), kind=kOutput, calls=%fused_computation.3 | convolution fusion | flops 4850707968 | bytes 41437184 | tf_op jit(solution)/shard_map/erf,edf->erd/dot_general | solution.py:388
  654.4 17.3 %multiply_convert_fusion = (bf16[8,576,1024]{2,1,0:T(8,128)(2,1)}, bf16[8,576,1024]{2,1,0:T(8,128)(2,1)}) fusion(f32[8,576]{1,0:T(8,128)S(1)} %mul.340, f32[4,8,144,1024]{3,2,0,1:T(8,128)} %copy.340, bf16[8,576,1024]{2,1,0:T(8,128)(2,1)} %get-tuple-element.180), kind=kLoop, calls=%fused_computation.5 | loop fusion | flops 23592960 | bytes 47204352 | tf_op jit(solution)/shard_map/convert_element_type | solution.py:400
  671.7 17.7 %multiply_convert_fusion.1 = (bf16[8,576,512]{2,1,0:T(8,128)(2,1)}, bf16[8,576,512]{2,1,0:T(8,128)(2,1)}) fusion(f32[8,576,512]{2,1,0:T(8,128)} %fusion.55, f32[8,576,512]{2,1,0:T(8,128)} %get-tuple-element.178, bf16[8,576,1024]{2,1,0:T(8,128)(2,1)} %get-tuple-element.36, bf16[8,1024,512]{2,1,0:T(8,128)(2,1)} %all-gather.15.cloned.1.call-done), kind=kOutput, calls=%fused_computation.10 | convolution fusion | flops 4862509056 | bytes 46137344 | tf_op jit(solution)/shard_map/erd,edf->erf/dot_general | solution.py:401
  689.5 12.7 fusion.56
  702.1 16.7 %add_convert_fusion = bf16[8,576,1024]{2,1,0:T(8,128)(2,1)} fusion(f32[8,576,1024]{2,1,0:T(8,128)} %fusion.56, bf16[8,576,512]{2,1,0:T(8,128)(2,1)} %get-tuple-element.35, bf16[8,1024,512]{2,1,0:T(8,128)(2,1)} %all-gather.13.cloned.1.call-done), kind=kOutput, calls=%fused_computation.4 | convolution fusion | flops 4841275392 | bytes 41418752 | tf_op jit(solution)/shard_map/erf,edf->erd/dot_general | solution.py:407
  718.8 9.2 copy.341
  727.9 10.9 convolution_convert_fusion.6
  738.9 6.5 copy.370
  745.5 7.7 maximum_maximum_fusion
  753.3 6.5 bitcast_convert_fusion
  759.8 9.6 copy.369
  771.0 74.6 %all-reduce.5.cloned.1.call-done = bf16[2048,1152]{0,1:T(8,128)(2,1)} async-done(((bf16[2048,1152]{0,1:T(8,128)(2,1)}), bf16[2048,1152]{0,1:T(8,128)(2,1)}) %all-reduce.5.cloned.1.call-update) | async-done | bytes 4718608 | tf_op jit(solution)/shard_map/psum | solution.py:421
  849.3 10.7 multiply_reduce_fusion.1
  860.8 7.3 multiply_add_fusion
  885.2 50.5 %shard_map.230 = (f32[4,2048,64]{2,1,0:T(8,128)S(1)}, f32[2,2048,64]{2,1,0:T(8,128)S(1)}, f32[2,2048,64]{2,1,0:T(8,128)S(1)}) custom-call(bf16[4,2048,64]{2,1,0:T(8,128)(2,1)S(1)} %copy-done.1, bf16[2,2048,64]{2,1,0:T(8,128)(2,1)S(1)} %copy-done.8, bf16[2,2048,64]{2,1,0:T(8,128)(2,1)S(1)} %bitcast.148, bf16[4,2048,64]{2,1,0:T(8,128)(2,1)S(1)} %bitcast.146, ...), custom_call_target="tpu_custom_call" | custom-call | flops 6442450944 | bytes 12582912 | tf_op jit(solution)/shard_map/pallas_call | solution.py:210
  951.4 8.5 fusion.54
  960.0 6.9 convolution_convert_fusion.9
  966.8 9.1 copy.352
  976.0 6.9 multiply_reduce_fusion
  989.2 9.3 copy.336
  998.5 11.3 convolution_convert_fusion.7
  1009.8 6.6 copy.368
  1016.4 39.1 %reduce-scatter.19.cloned.1.call-done = bf16[128,896]{1,0:T(8,128)(2,1)} async-done(((bf16[1024,896]{1,0:T(8,128)(2,1)}), bf16[128,896]{1,0:T(8,128)(2,1)}) %reduce-scatter.19.cloned.1.call-update) | async-done | bytes 229392
  1060.7 13.5 convolution_convert_fusion.2
  1074.2 13.6 convolution_convert_fusion.3
  1087.8 13.0 convolution_convert_fusion.4
  1110.8 38.7 %reduce-scatter.21.cloned.1.call-done = bf16[528,1024]{1,0:T(8,128)(2,1)} async-done(((bf16[2112,1024]{1,0:T(8,128)(2,1)}), bf16[528,1024]{1,0:T(8,128)(2,1)}) %reduce-scatter.21.cloned.1.call-update) | async-done | bytes 1081360
  1160.9 141.8 %reduce-scatter.17.cloned.1.call-done = bf16[8,128,512]{2,1,0:T(8,128)(2,1)} async-done(((bf16[8,1024,512]{2,1,0:T(8,128)(2,1)}), bf16[8,128,512]{2,1,0:T(8,128)(2,1)}) %reduce-scatter.17.cloned.1.call-update) | async-done | bytes 1048592 | tf_op jit(solution)/shard_map/reduce_scatter | solution.py:431
  1306.0 148.3 %reduce-scatter.15.cloned.1.call-done = bf16[8,128,512]{2,1,0:T(8,128)(2,1)} async-done(((bf16[8,1024,512]{2,1,0:T(8,128)(2,1)}), bf16[8,128,512]{2,1,0:T(8,128)(2,1)}) %reduce-scatter.15.cloned.1.call-update) | async-done | bytes 1048592 | tf_op jit(solution)/shard_map/reduce_scatter | solution.py:427
  1457.1 149.3 %reduce-scatter.13.cloned.1.call-done = bf16[8,128,512]{2,1,0:T(8,128)(2,1)} async-done(((bf16[8,1024,512]{2,1,0:T(8,128)(2,1)}), bf16[8,128,512]{2,1,0:T(8,128)(2,1)}) %reduce-scatter.13.cloned.1.call-update) | async-done | bytes 1048592 | tf_op jit(solution)/shard_map/reduce_scatter | solution.py:423
  (298 shorter events, 153.3 us)
Async XLA Ops:
  7.2 7.6 copy-start.54
  7.2 7.7 copy-start.59
  7.2 7.9 copy-start.60
  7.2 70.9 %all-gather.17.cloned.1.call-start = ((), (), s32[]{:S(2)}) async-start(), calls=%async_computation.15 | async-start | bytes 10977280 | tf_op jit(solution)/shard_map/all_gather | solution.py:291
  14.7 66.7 %copy-start.13 = (s32[2048]{0:T(1024)S(1)}, s32[2048]{0:T(1024)}, u32[]{:S(2)}) copy-start(s32[2048]{0:T(1024)} %param.16) | copy-start | bytes 24580
  14.7 132.0 %all-gather.19.cloned.1.call-start = ((), (), s32[]{:S(2)}) async-start(), calls=%async_computation.16 | async-start | bytes 3981312 | tf_op jit(solution)/shard_map/all_gather | solution.py:303
  81.4 174.3 %all-gather.9.cloned.1.call-start = ((), (), s32[]{:S(2)}) async-start(), calls=%async_computation.6 | async-start | bytes 5242880 | tf_op jit(solution)/shard_map/all_gather | solution.py:337
  90.8 80.9 %copy-start.20 = (f32[2048,32]{1,0:T(8,128)}, f32[2048,32]{1,0:T(8,128)S(1)}, u32[]{:S(2)}) copy-start(f32[2048,32]{1,0:T(8,128)S(1)} %get-tuple-element.174) | copy-start | bytes 786436
  111.1 48.0 %copy-start.57 = (f32[1,4,4,128]{3,1,2,0:T(4,128)}, f32[1,4,4,128]{3,1,2,0:T(4,128)S(1)}, u32[]{:S(2)}) copy-start(f32[1,4,4,128]{3,1,2,0:T(4,128)S(1)} %copy.379) | copy-start | bytes 24580
  151.9 7.1 copy-start.46
  178.9 39.5 %copy-start.7 = (bf16[2,2048,64]{2,1,0:T(8,128)(2,1)}, bf16[2,2048,64]{2,1,0:T(8,128)(2,1)S(1)}, u32[]{:S(2)}) copy-start(bf16[2,2048,64]{2,1,0:T(8,128)(2,1)S(1)} %pad_maximum_fusion.3.k_ref) | copy-start | bytes 1572868
  180.1 38.3 %copy-start = (bf16[4,2048,64]{2,1,0:T(8,128)(2,1)}, bf16[4,2048,64]{2,1,0:T(8,128)(2,1)S(1)}, u32[]{:S(2)}) copy-start(bf16[4,2048,64]{2,1,0:T(8,128)(2,1)S(1)} %pad_maximum_fusion.1.q_ref) | copy-start | bytes 3145732
  222.6 160.1 %all-gather.11.cloned.1.call-start = ((), (), s32[]{:S(2)}) async-start(), calls=%async_computation.7 | async-start | bytes 9437184 | tf_op jit(solution)/shard_map/all_gather | solution.py:318
  224.0 283.8 %all-gather.13.cloned.1.call-start = ((), (), s32[]{:S(2)}) async-start(), calls=%async_computation.8 | async-start | bytes 9437184 | tf_op jit(solution)/shard_map/all_gather | solution.py:319
  224.6 409.0 %all-gather.15.cloned.1.call-start = ((), (), s32[]{:S(2)}) async-start(), calls=%async_computation.9 | async-start | bytes 9437184 | tf_op jit(solution)/shard_map/all_gather | solution.py:320
  225.2 620.4 %all-reduce.5.cloned.1.call-start = ((), (), s32[]{:S(2)}) async-start(), calls=%async_computation.11 | async-start | bytes 9437184 | tf_op jit(solution)/shard_map/psum | solution.py:421
  229.6 10.6 copy-start.39
  240.1 12.9 copy-start.53
  240.1 12.9 slice-start.2
  240.1 15.6 copy-start.25
  253.1 10.9 copy-start.51
  253.2 42.7 %copy-start.37 = (bf16[1024,32]{1,0:T(8,128)(2,1)}, bf16[1024,32]{1,0:T(8,128)(2,1)S(1)}, u32[]{:S(2)}) copy-start(bf16[1024,32]{1,0:T(8,128)(2,1)S(1)} %reshape.396) | copy-start | bytes 196612
  633.6 16.8 %copy-start.48 = (s32[4,8,512]{2,1,0:T(8,128)S(1)}, s32[4,8,512]{2,1,0:T(8,128)}, u32[]{:S(2)}) copy-start(s32[4,8,512]{2,1,0:T(8,128)} %copy-done.47) | copy-start | bytes 196612
  738.9 6.6 copy-start.61
  753.3 302.3 %reduce-scatter.19.cloned.1.call-start = ((), (), s32[]{:S(2)}) async-start(), calls=%async_computation.17 | async-start | bytes 2064384
  759.8 9.6 copy-start.26
  771.0 78.1 %copy-start.36 = (f32[2048,32]{0,1:T(8,128)S(1)}, f32[2048,32]{0,1:T(8,128)}, u32[]{:S(2)}) copy-start(f32[2048,32]{0,1:T(8,128)} %copy-done.35) | copy-start | bytes 786436
  771.0 78.3 %copy-start.38 = (bf16[1024,32]{1,0:T(8,128)(2,1)S(1)}, bf16[1024,32]{1,0:T(8,128)(2,1)}, u32[]{:S(2)}) copy-start(bf16[1024,32]{1,0:T(8,128)(2,1)} %copy-done.37) | copy-start | bytes 196612
  771.0 78.3 %copy-start.50 = (f32[2048]{0:T(1024)S(1)}, f32[2048]{0:T(1024)}, u32[]{:S(2)}) copy-start(f32[2048]{0:T(1024)} %copy-done.49) | copy-start | bytes 24580
  771.0 78.3 %copy-start.52 = (f32[1024]{0:T(1024)S(1)}, f32[1024]{0:T(1024)}, u32[]{:S(2)}) copy-start(f32[1024]{0:T(1024)} %copy-done.51) | copy-start | bytes 12292
  849.3 11.5 slice-start
  849.3 11.4 slice-start.1
  860.8 7.3 copy-start.28
  885.2 50.6 %copy-start.21 = (f32[2048,32]{1,0:T(8,128)S(1)}, f32[2048,32]{1,0:T(8,128)}, u32[]{:S(2)}) copy-start(f32[2048,32]{1,0:T(8,128)} %copy-done.20) | copy-start | bytes 786436
  885.2 50.6 %copy-start.27 = (f32[2048,32]{1,0:T(8,128)S(1)}, f32[2048,32]{1,0:T(8,128)}, u32[]{:S(2)}) copy-start(f32[2048,32]{1,0:T(8,128)} %get-tuple-element.172) | copy-start | bytes 786436
  944.8 6.6 copy-start.32
  951.4 8.6 copy-start.42
  951.4 8.6 copy-start.56
  951.4 8.6 copy-start.58
  976.0 7.0 copy-start.18
  976.0 7.0 copy-start.45
  989.1 118.1 %reduce-scatter.11.cloned.1.call-start = ((), (), s32[]{:S(2)}) async-start(), calls=%async_computation.10 | async-start | bytes 5242880 | tf_op jit(solution)/shard_map/reduce_scatter | solution.py:395
  989.2 9.3 copy-start.41
  1016.4 133.1 %reduce-scatter.21.cloned.1.call-start = ((), (), s32[]{:S(2)}) async-start(), calls=%async_computation.18 | async-start | bytes 5406720
  1060.6 242.1 %reduce-scatter.17.cloned.1.call-start = ((), (), s32[]{:S(2)}) async-start(), calls=%async_computation.14 | async-start | bytes 9437184 | tf_op jit(solution)/shard_map/reduce_scatter | solution.py:431
  1074.1 380.1 %reduce-scatter.15.cloned.1.call-start = ((), (), s32[]{:S(2)}) async-start(), calls=%async_computation.13 | async-start | bytes 9437184 | tf_op jit(solution)/shard_map/reduce_scatter | solution.py:427
  1087.8 518.6 %reduce-scatter.13.cloned.1.call-start = ((), (), s32[]{:S(2)}) async-start(), calls=%async_computation.12 | async-start | bytes 9437184 | tf_op jit(solution)/shard_map/reduce_scatter | solution.py:423
  1102.6 8.2 copy-start.23
  (30 other events, 87.7 us)
Sparse Core Ops, SparseCore 0:
  14.9 63.2 all-gather.16
  81.5 65.1 all-gather.18
  222.7 32.9 all-gather.8
  257.8 124.9 all-gather.10
  384.7 123.0 all-gather.12
  510.5 123.0 all-gather.14
  753.4 92.1 all-reduce.4
  989.3 66.2 reduce-scatter.18
  1058.3 43.3 reduce-scatter.10
  1104.1 45.3 reduce-scatter.20
  1153.6 149.0 reduce-scatter.16
  1306.1 148.0 reduce-scatter.14
  1458.3 148.0 reduce-scatter.12
